TPU v7x, 32 devices: a whole 2x2x4 slice. The times are simulated.
32 devices in a mesh: img: 8 (over y, x, core), blk: 4 (over z).
Axes of the slice: x: 2, y: 2, z: 4, core: 2. Of those that a mesh axis runs over, the one named last changes fastest.
Arguments:
- images: bfloat16 [32, 28, 1792], P('img'), may hold values from -6 to 6
- filters: bfloat16 [2048, 576], P('blk'), may hold values from -0.5 to 0.5
- phases: float32 [2048], P('blk'), may hold values from -3.140625 to 3.140625
- labels: int32 [6272], P('img'), may hold values from 0 to 149
- weights: float32 [150, 2048], P(None, 'blk'), may hold values from -6 to 6
Outputs:
- new_weights: float32 [150, 2048], P(None, 'blk')
- residual: float32 [150, 6272], P(None, 'img')
All inputs are finite; a program needn't handle non-finite values.
Results may differ from a plain program's by a relative error of at most 0.015.
Values may be sent and summed in bfloat16 or wider, within the bound.
A program may use at most 64 MiB of HBM per device.

v0:
```python
import math

import jax
import jax.numpy as jnp
from jax import lax
from jax.sharding import PartitionSpec as P

SIDE = 28
CHAN = 64
FILT = 512
LABELS = 150
ITERS = 2


RIDGE = 0.5
DAMPING = 0.75


def block_features(images, filter_rows, phase_rows):
    count_images = images.shape[0]
    pictures = images.reshape(count_images, SIDE, SIDE, CHAN)
    kernel = filter_rows.reshape(filter_rows.shape[0], 3, 3, CHAN)
    response = lax.conv_general_dilated(
        pictures,
        kernel,
        (2, 2),
        ((1, 1), (1, 1)),
        dimension_numbers=("NHWC", "OHWI", "CNHW"),
        preferred_element_type=jnp.float32,
    )
    response = response.reshape(filter_rows.shape[0], count_images * (SIDE // 2) ** 2)
    return (math.sqrt(2.0) * jnp.cos(response + phase_rows[:, None])).astype(jnp.bfloat16)


def solve_with(factor, projected):
    middle = lax.linalg.triangular_solve(
        factor, projected, left_side=False, lower=True, transpose_a=True
    )
    return lax.linalg.triangular_solve(
        factor, middle, left_side=False, lower=True, transpose_a=False
    )


def predict(weight_now, features, shrink):
    partial_value = shrink * jnp.dot(
        weight_now.astype(jnp.bfloat16), features, preferred_element_type=jnp.float32
    )
    return lax.psum(partial_value.astype(jnp.bfloat16), "blk").astype(jnp.float32)


def shards(images, filters, phases, labels, weights):
    features = block_features(images, filters, phases)
    image_groups = lax.axis_size("img")
    pixels = labels.shape[0] * image_groups
    features_all = FILT * lax.axis_size("blk")
    shrink = 1.0 / math.sqrt(features_all)
    expand = math.sqrt(features_all)
    targets = (labels[None, :] == jnp.arange(LABELS, dtype=jnp.int32)[:, None]).astype(jnp.float32)
    identity = jnp.eye(FILT, dtype=jnp.float32)
    local_gram = lax.dot_general(
        features, features, (((1,), (1,)), ((), ())), preferred_element_type=jnp.float32
    )
    predicted = predict(weights, features, shrink)
    gram = lax.psum(local_gram, "img") + RIDGE * pixels * identity
    factor = jnp.linalg.cholesky(gram)
    residual = targets - predicted
    weight_now = weights
    for step in range(ITERS):
        local_projection = lax.dot_general(
            residual.astype(jnp.bfloat16),
            features,
            (((1,), (1,)), ((), ())),
            preferred_element_type=jnp.float32,
        )
        projected = lax.psum(local_projection, "img")
        weight_now = weight_now + DAMPING * (expand * solve_with(factor, projected))
        residual = targets - predict(weight_now, features, shrink)
    return (weight_now, residual)


def solution(mesh):
    return jax.shard_map(
        shards,
        mesh=mesh,
        in_specs=(P("img", None, None), P("blk", None), P("blk"), P("img"), P(None, "blk")),
        out_specs=(P(None, "blk"), P(None, "img")),
        check_vma=False,
    )
```

profile of v0, /device:TPU:0, one launch (start us, length us, event | category | flops | bytes accessed | tf_op | source)
XLA Modules:
  0.0 429.0 jit_solution(3119237284669562733)
XLA Ops:
  7.2 1.9 reshape.77
  9.1 14.1 %multiply_convert_fusion.1 = (bf16[512,4,14,14]{0,1,3,2:T(4,128)(2,1)}, f32[512,4,14,14]{0,1,3,2:T(4,128)S(1)}) fusion(f32[512]{0:T(512)} %param.11, bf16[512,3,3,64]{0,3,2,1:T(8,128)(2,1)S(1)} %bitcast.114, bf16[4,28,28,64]{3,2,0,1:T(8,128)(2,1)S(1)} %reshape.77), kind=kOutput, calls=%fused_computation.3 | convolution fusion | flops 441868288 | bytes 3401728 | tf_op jit(solution)/shard_map/conv_general_dilated | solution.py:23
  25.1 6.4 %multiply_convert_fusion = bf16[512,784]{0,1:T(8,128)(2,1)S(1)} fusion(f32[512,784]{0,1:T(8,128)} %reshape.79, f32[512]{0:T(512)S(1)} %copy-done.8), kind=kLoop, calls=%fused_computation.2 | loop fusion | flops 1204224 | bytes 2410496 | tf_op jit(solution)/shard_map/convert_element_type | solution.py:32
  32.8 1.8 convolution_bitcast_fusion
  34.6 36.5 %all-reduce.8.cloned.1.call-done = bf16[150,784]{1,0:T(8,128)(2,1)} async-done(((bf16[150,784]{1,0:T(8,128)(2,1)}), bf16[150,784]{1,0:T(8,128)(2,1)}) %all-reduce.8.cloned.1.call-update) | async-done | bytes 235216 | tf_op jit(solution)/shard_map/psum | solution.py:48
  71.1 2.0 fusion.14
  73.3 59.7 %all-reduce.16.cloned.1.call-done = (f32[150,512]{1,0:T(8,128)}, f32[512,512]{0,1:T(8,128)}) async-done(((f32[150,512]{1,0:T(8,128)}, f32[512,512]{0,1:T(8,128)}), (f32[150,512]{1,0:T(8,128)}, f32[512,512]{0,1:T(8,128)})) %all-reduce.16.cloned.1.call-update) | async-done | bytes 1355792 | tf_op jit(solution)/shard_map/psum | solution.py:75
  133.1 2.5 select_add_fusion
  135.5 1.6 copy.27
  138.3 11.7 %cholesky.103 = f32[128,128]{1,0:T(8,128)S(1)} custom-call(f32[128,128]{1,0:T(8,128)S(1)} %cholesky.263), custom_call_target="Cholesky" | custom-call | tf_op jit(solution)/shard_map/jit(cholesky)/cholesky | solution.py:65
  150.2 9.8 %custom-call.33 = f32[1,128,128]{1,2,0:T(8,128)S(1)} custom-call(f32[1,128,128]{2,1,0:T(8,128)S(1)} %get-tuple-element.85), custom_call_target="InvertDiagBlocksLowerTriangular" | custom-call | tf_op jit(solution)/shard_map/jit(cholesky)/cholesky | solution.py:65
  162.7 11.7 %cholesky.215 = f32[128,128]{1,0:T(8,128)S(1)} custom-call(f32[128,128]{1,0:T(8,128)S(1)} %cholesky.267), custom_call_target="Cholesky" | custom-call | tf_op jit(solution)/shard_map/jit(cholesky)/cholesky | solution.py:65
  174.5 10.0 %custom-call.34 = f32[1,128,128]{1,2,0:T(8,128)S(1)} custom-call(f32[1,128,128]{2,1,0:T(8,128)S(1)} %get-tuple-element.83), custom_call_target="InvertDiagBlocksLowerTriangular" | custom-call | tf_op jit(solution)/shard_map/jit(cholesky)/cholesky | solution.py:65
  185.0 1.5 convolution_subtract_fusion.1
  186.5 11.7 %cholesky.236 = f32[128,128]{1,0:T(8,128)S(1)} custom-call(f32[128,128]{1,0:T(8,128)S(1)} %cholesky.272), custom_call_target="Cholesky" | custom-call | tf_op jit(solution)/shard_map/jit(cholesky)/cholesky | solution.py:65
  198.4 9.8 %custom-call.35 = f32[1,128,128]{1,2,0:T(8,128)S(1)} custom-call(f32[1,128,128]{2,1,0:T(8,128)S(1)} %get-tuple-element.81), custom_call_target="InvertDiagBlocksLowerTriangular" | custom-call | tf_op jit(solution)/shard_map/jit(cholesky)/cholesky | solution.py:65
  209.8 11.9 %cholesky.253 = f32[128,128]{1,0:T(8,128)S(1)} custom-call(f32[128,128]{1,0:T(8,128)S(1)} %convolution_subtract_fusion.14), custom_call_target="Cholesky" | custom-call | tf_op jit(solution)/shard_map/jit(cholesky)/cholesky | solution.py:65
  226.6 11.4 %while.8 = (s32[]{:T(128)}, f32[512,512]{0,1:T(8,128)S(1)}, s32[4,2]{0,1:T(2,128)S(1)}, f32[4,128,128]{2,1,0:T(8,128)}, s32[]{:T(128)}) while((s32[]{:T(128)}, f32[512,512]{0,1:T(8,128)S(1)}, s32[4,2]{0,1:T(2,128)S(1)}, f32[4,128,128]{2,1,0:T(8,128)}, s32[]{:T(128)}) %tuple.49), condition=%wide.while_cond, body=%wide.while_body.sunk | while | flops 2 | bytes 393329 | solution.py:36
  238.0 40.1 %custom-call.38 = f32[4,128,128]{1,2,0:T(8,128)S(1)} custom-call(f32[4,128,128]{2,1,0:T(8,128)} %get-tuple-element.32), custom_call_target="InvertDiagBlocksLowerTriangular" | custom-call | tf_op jit(solution)/shard_map/triangular_solve/custom-call.3 | solution.py:36
  283.8 34.8 %all-reduce.10.cloned.1.call-done = bf16[150,784]{1,0:T(8,128)(2,1)} async-done(((bf16[150,784]{1,0:T(8,128)(2,1)}), bf16[150,784]{1,0:T(8,128)(2,1)}) %all-reduce.10.cloned.1.call-update) | async-done | bytes 235216 | tf_op jit(solution)/shard_map/psum | solution.py:48
  318.6 2.0 fusion.12
  320.7 55.2 %all-reduce.12.cloned.1.call-done = f32[150,512]{1,0:T(8,128)} async-done(((f32[150,512]{1,0:T(8,128)}), f32[150,512]{1,0:T(8,128)}) %all-reduce.12.cloned.1.call-update) | async-done | bytes 307216 | tf_op jit(solution)/shard_map/psum | solution.py:75
  385.1 35.1 %all-reduce.14.cloned.1.call-done = bf16[150,784]{1,0:T(8,128)(2,1)} async-done(((bf16[150,784]{1,0:T(8,128)(2,1)}), bf16[150,784]{1,0:T(8,128)(2,1)}) %all-reduce.14.cloned.1.call-update) | async-done | bytes 235216 | tf_op jit(solution)/shard_map/psum | solution.py:48
  420.2 1.8 convert_subtract_fusion
  (114 shorter events, 38.0 us)
Async XLA Ops:
  7.2 2.0 copy-start
  7.2 63.9 %all-reduce.8.cloned.1.call-start = ((), (), s32[]{:S(2)}) async-start(), calls=%async_computation | async-start | bytes 544768 | tf_op jit(solution)/shard_map/psum | solution.py:48
  23.8 1.4 copy-start.8
  25.1 6.4 %copy-start.2 = (f32[150,512]{1,0:T(8,128)S(1)}, f32[150,512]{1,0:T(8,128)}, u32[]{:S(2)}) copy-start(f32[150,512]{1,0:T(8,128)} %param.13) | copy-start | bytes 921604
  25.1 7.7 %copy-start.9 = (bf16[512,4,14,14]{0,1,3,2:T(4,128)(2,1)S(1)}, bf16[512,4,14,14]{0,1,3,2:T(4,128)(2,1)}, u32[]{:S(2)}) copy-start(bf16[512,4,14,14]{0,1,3,2:T(4,128)(2,1)} %get-tuple-element.86) | copy-start | bytes 2408452
  32.7 38.3 %copy-start.7 = (s32[784]{0:T(1024)S(1)}, s32[784]{0:T(1024)}, u32[]{:S(2)}) copy-start(s32[784]{0:T(1024)} %param.12) | copy-start | bytes 9412
  32.7 100.3 %all-reduce.16.cloned.1.call-start = ((), (), s32[]{:S(2)}) async-start(), calls=%async_computation.4 | async-start | bytes 2719744 | tf_op jit(solution)/shard_map/psum | solution.py:75
  73.1 245.5 %all-reduce.10.cloned.1.call-start = ((), (), s32[]{:S(2)}) async-start(), calls=%async_computation.1 | async-start | bytes 544768 | tf_op jit(solution)/shard_map/psum | solution.py:48
  133.1 4.0 copy-start.1
  137.3 1.0 copy-start.4
  226.6 51.5 %copy-start.6 = (f32[150,512]{1,0:T(8,128)S(1)}, f32[150,512]{1,0:T(8,128)}, u32[]{:S(2)}) copy-start(f32[150,512]{1,0:T(8,128)} %get-tuple-element.76) | copy-start | bytes 921604
  279.3 3.2 copy-start.3
  283.7 92.2 %all-reduce.12.cloned.1.call-start = ((), (), s32[]{:S(2)}) async-start(), calls=%async_computation.2 | async-start | bytes 622592 | tf_op jit(solution)/shard_map/psum | solution.py:75
  320.6 99.6 %all-reduce.14.cloned.1.call-start = ((), (), s32[]{:S(2)}) async-start(), calls=%async_computation.3 | async-start | bytes 544768 | tf_op jit(solution)/shard_map/psum | solution.py:48
  383.9 38.2 %copy-start.5 = (f32[150,512]{1,0:T(8,128)}, f32[150,512]{1,0:T(8,128)S(1)}, u32[]{:S(2)}) copy-start(f32[150,512]{1,0:T(8,128)S(1)} %fusion.11) | copy-start | bytes 921604
Sparse Core Ops, SparseCore 0:
  32.9 38.1 all-reduce.7
  74.9 58.0 all-reduce.15
  283.8 34.7 all-reduce.9
  322.1 53.7 all-reduce.11
  385.2 34.9 all-reduce.13
where the time goes:
time: 435 us; the launch traced here: 429 us
  waiting for transfers between devices  221 us (51%)
  other arithmetic  130 us (30%)
  matrix products  41.5 us (10%)
  local copies, waits for them, and re-layouts  18.3 us (4%)
  between operations  17.3 us (4%)
    psum x2, waiting for transfers between devices, shards(): projected = lax.psum(local_projection, 'img')  115 us
    psum x3, waiting for transfers between devices, predict(): lax.psum(partial_value.astype(jnp.bfloat16), 'blk').astype(jnp.float32)  106 us
    another operation x14, other arithmetic, shards(): factor = jnp.linalg.cholesky(gram)  78.8 us
    another operation x4, other arithmetic, solve_with(): lax.linalg.triangular_solve(factor, projected, left_side=False, lower=Tru...  40.3 us
    conv_general_dilated x1, matrix products, block_features(): lax.conv_general_dilated(pictures, kernel, (2, 2), ((1, 1), (1, 1)), dime...  14.1 us
    another operation x21, local copies, waits for them, and re-layouts, solve_with(): lax.linalg.triangular_solve(factor, projected, left_side=False, lower=Tru...  11.3 us
  transfers between devices with their start and end apart: 5, of which 5 were waited for; matrix products, arithmetic and copies ran while one was open for 0% of the time, Pallas kernels for 0%

commit v1 on v0

v1 whole, which is shorter than its diff:
```python
import math

import jax
import jax.numpy as jnp
import numpy as np
from jax import lax
from jax.experimental import pallas as pl
from jax.experimental.pallas import tpu as pltpu
from jax.sharding import PartitionSpec as P

SIDE = 28
CHAN = 64
LABELS = 150
ITERS = 2
RIDGE = 0.5
DAMPING = 0.75
TILE = 128


def cosine_coefficients(degree=6):
    nodes = np.cos((np.arange(400) + 0.5) * np.pi / 400)
    square = (nodes + 1.0) * (np.pi**2 * 1.0005) / 2
    fit = np.polynomial.chebyshev.Chebyshev.fit(square, np.sqrt(2.0) * np.cos(np.sqrt(square)), degree)
    return [float(c) for c in fit.convert(kind=np.polynomial.Polynomial).coef]


COEFFICIENTS = cosine_coefficients()
TURN_HIGH = 6.28125
TURN_LOW = 2.0 * math.pi - TURN_HIGH


def inverse_scales(lowest):
    scales = []
    while 1.0 - lowest > 1e-6:
        scale = 2.0 / (1.0 + lowest)
        scales.append(scale)
        lowest = scale * lowest * (2.0 - scale * lowest)
    return scales


def split(value):
    high = value.astype(jnp.bfloat16)
    return high, (value - high.astype(jnp.float32)).astype(jnp.bfloat16)


def dot(a, b):
    return jnp.dot(a, b, preferred_element_type=jnp.float32)


def dot_nt(a, b):
    return lax.dot_general(a, b, (((1,), (1,)), ((), ())), preferred_element_type=jnp.float32)


def dot_three(a_high, a_low, b_high, b_low):
    return dot(a_high, b_high) + (dot(a_high, b_low) + dot(a_low, b_high))


def make_kernel(n_img, n_blk, filt, pos, pos_pad, pixels, rows_img, rows_blk, rows_all):
    features_all = filt * n_blk
    shrink = 1.0 / math.sqrt(features_all)
    expand = math.sqrt(features_all)
    tiles = filt // TILE
    packed = tiles * (tiles + 1) // 2 * TILE
    rows_gram = packed // n_img
    upper = (RIDGE + 2.0 * filt) * pixels
    scales = inverse_scales(RIDGE * pixels / upper)

    def kernel(
        patches_ref, filters_ref, phases_ref, labels_ref, weights_ref, scales_ref,
        out_weights, out_residual,
        feat, gram, gram_in, gram_all, h_high, h_low, x_now, x_high, x_low, y_high, y_low,
        part, part_in, part_all, resid, proj, proj_in, w_own, w_all,
        gram_s, gram_r, gram_all_s, gram_all_r,
        part_s, part_r, part_all_s, part_all_r,
        proj_s, proj_r, w_s, w_r,
    ):
        img = lax.axis_index("img")
        blk = lax.axis_index("blk")
        barrier = pltpu.get_barrier_semaphore()

        def each_peer(me, n, body):
            def one(step, carry):
                body(step, lax.rem(me + step, n))
                return carry

            lax.fori_loop(1, n, one, 0)

        each_peer(img, n_img, lambda step, peer: pl.semaphore_signal(
            barrier, inc=1, device_id={"img": peer}, device_id_type=pl.DeviceIdType.MESH))
        each_peer(blk, n_blk, lambda step, peer: pl.semaphore_signal(
            barrier, inc=1, device_id={"blk": peer}, device_id_type=pl.DeviceIdType.MESH))

        def scatter(axis, me, n, rows, source, target, send, recv):
            def copy(step, peer, slot):
                return pltpu.make_async_remote_copy(
                    src_ref=source.at[pl.ds(pl.multiple_of(peer * rows, 8), rows)],
                    dst_ref=target.at[slot],
                    send_sem=send.at[step], recv_sem=recv.at[slot],
                    device_id={axis: peer}, device_id_type=pl.DeviceIdType.MESH)

            def start():
                each_peer(me, n, lambda step, peer: copy(step, peer, me).start())
                target[me] = source[pl.ds(pl.multiple_of(me * rows, 8), rows), :]

            def wait():
                each_peer(me, n, lambda step, peer: copy(step, peer, peer).wait_recv())

            def wait_sent():
                each_peer(me, n, lambda step, peer: copy(step, peer, me).wait_send())

            return start, wait, wait_sent

        def gather(axis, me, n, rows, whole, send, recv):
            def copy(step, peer, slot):
                place = whole.at[pl.ds(pl.multiple_of(slot * rows, 8), rows)]
                return pltpu.make_async_remote_copy(
                    src_ref=place, dst_ref=place,
                    send_sem=send.at[step], recv_sem=recv.at[slot],
                    device_id={axis: peer}, device_id_type=pl.DeviceIdType.MESH)

            def start(value):
                whole[pl.ds(pl.multiple_of(me * rows, 8), rows), :] = value
                each_peer(me, n, lambda step, peer: copy(step, peer, me).start())

            def wait():
                each_peer(me, n, lambda step, peer: copy(step, peer, peer).wait_recv())

            def wait_sent():
                each_peer(me, n, lambda step, peer: copy(step, peer, me).wait_send())

            return start, wait, wait_sent

        unsent = []

        inside = lax.broadcasted_iota(jnp.int32, (TILE, pos_pad), 1) < pos
        for tile in range(tiles):
            here = slice(tile * TILE, (tile + 1) * TILE)
            angle = dot_nt(filters_ref[here, :], patches_ref[...]) + phases_ref[here, :]
            turns = jnp.floor(angle * (0.5 / math.pi) + 0.5)
            angle = (angle - turns * TURN_HIGH) - turns * TURN_LOW
            square = angle * angle
            value = jnp.full_like(square, COEFFICIENTS[-1])
            for coefficient in COEFFICIENTS[-2::-1]:
                value = value * square + coefficient
            feat[here, :] = jnp.where(inside, value, 0.0).astype(jnp.bfloat16)

        spot = 0
        for row in range(tiles):
            block = dot_nt(feat[row * TILE:(row + 1) * TILE, :], feat[: (row + 1) * TILE, :])
            for col in range(row + 1):
                gram[spot * TILE:(spot + 1) * TILE, :] = block[:, col * TILE:(col + 1) * TILE]
                spot += 1

        pl.semaphore_wait(barrier, n_img - 1 + n_blk - 1)
        gram_scatter = scatter("img", img, n_img, rows_gram, gram, gram_in, gram_s, gram_r)
        gram_gather = gather("img", img, n_img, rows_gram, gram_all, gram_all_s, gram_all_r)
        gram_scatter[0]()

        def begin_predict(turn, weight_now):
            send = scatter("blk", blk, n_blk, rows_blk, part.at[turn], part_in.at[turn],
                           part_s.at[turn], part_r.at[turn])
            part[turn] = (shrink * dot(weight_now, feat[...])).astype(jnp.bfloat16)
            send[0]()
            return send

        def middle_predict(turn, send):
            share = gather("blk", blk, n_blk, rows_blk, part_all.at[turn],
                           part_all_s.at[turn], part_all_r.at[turn])
            send[1]()
            total = jnp.sum(part_in[turn].astype(jnp.float32), axis=0)
            share[0](total.astype(jnp.bfloat16))
            unsent.extend([send[2], share[2]])
            return share

        def end_predict(turn, share):
            share[1]()
            classes = lax.broadcasted_iota(jnp.int32, (rows_all, pos_pad), 0)
            targets = jnp.where(labels_ref[...] == classes, 1.0, 0.0)
            return targets - part_all[turn].astype(jnp.float32)

        def begin_project(step):
            send = scatter("img", img, n_img, rows_img, proj.at[step], proj_in.at[step],
                           proj_s.at[step], proj_r.at[step])
            proj[step] = dot_nt(resid[...], feat[...])
            send[0]()
            return send

        def solve_step(step, send):
            send[1]()
            p_high, p_low = split(jnp.sum(proj_in[step], axis=0))
            change = expand * dot_three(p_high, p_low, x_high[...], x_low[...])
            w_own[...] += DAMPING * change
            share = gather("img", img, n_img, rows_img, w_all.at[step], w_s.at[step], w_r.at[step])
            share[0](w_own[...])
            share[1]()
            unsent.extend([send[2], share[2]])

        predict_send = begin_predict(0, weights_ref[...].astype(jnp.bfloat16))
        w_own[...] = weights_ref[pl.ds(pl.multiple_of(img * rows_img, 8), rows_img), :]
        if rows_all > n_img * rows_img:
            for step in range(ITERS):
                w_all[step] = jnp.zeros((rows_all, filt), jnp.float32)

        gram_scatter[1]()
        gram_gather[0](jnp.sum(gram_in[...], axis=0))
        unsent.extend([gram_scatter[2], gram_gather[2]])
        share = middle_predict(0, predict_send)
        gram_gather[1]()

        spot = 0
        diagonal = (lax.broadcasted_iota(jnp.int32, (TILE, TILE), 0)
                    == lax.broadcasted_iota(jnp.int32, (TILE, TILE), 1))
        first = scales[0]
        for row in range(tiles):
            for col in range(row + 1):
                block = gram_all[spot * TILE:(spot + 1) * TILE, :]
                spot += 1
                if row == col:
                    block = block + jnp.where(diagonal, RIDGE * pixels, 0.0)
                start = block * (-first * first / upper / upper)
                if row == col:
                    start = start + jnp.where(diagonal, 2.0 * first / upper, 0.0)
                places = [(row, col, block, start)]
                if row != col:
                    places.append((col, row, block.T, start.T))
                for down, across, h_part, x_part in places:
                    at = (slice(down * TILE, (down + 1) * TILE), slice(across * TILE, (across + 1) * TILE))
                    h_high[at], h_low[at] = split(h_part)
                    x_now[at] = x_part
                    x_high[at], x_low[at] = split(x_part)

        resid[...] = end_predict(0, share).astype(jnp.bfloat16)
        project_send = begin_project(0)

        def newton(step, carry):
            scale = scales_ref[step]
            y = dot_three(h_high[...], h_low[...], x_high[...], x_low[...]) * (-scale)
            same = (lax.broadcasted_iota(jnp.int32, (filt, filt), 0)
                    == lax.broadcasted_iota(jnp.int32, (filt, filt), 1))
            y_high[...], y_low[...] = split(y + jnp.where(same, 2.0, 0.0))
            x = dot_three(x_high[...], x_low[...], y_high[...], y_low[...]) * scale
            x_high[...], x_low[...] = split(x)
            return carry

        lax.fori_loop(1, len(scales), newton, 0)

        for step in range(ITERS):
            solve_step(step, project_send)
            send = begin_predict(step + 1, w_all[step].astype(jnp.bfloat16))
            if step == ITERS - 1:
                out_weights[...] = w_all[step, :LABELS, :]
            share = middle_predict(step + 1, send)
            residual = end_predict(step + 1, share)
            if step < ITERS - 1:
                resid[...] = residual.astype(jnp.bfloat16)
                project_send = begin_project(step + 1)
            else:
                out_residual[...] = residual[:LABELS, :pos]
        for wait_sent in unsent:
            wait_sent()

    f32, bf16 = jnp.float32, jnp.bfloat16
    square = (filt, filt)
    dma = pltpu.SemaphoreType.DMA
    turns = ITERS + 1
    scratch = [
        pltpu.VMEM((filt, pos_pad), bf16),
        pltpu.VMEM((packed, TILE), f32),
        pltpu.VMEM((n_img, rows_gram, TILE), f32),
        pltpu.VMEM((packed, TILE), f32),
        pltpu.VMEM(square, bf16), pltpu.VMEM(square, bf16),
        pltpu.VMEM(square, f32), pltpu.VMEM(square, bf16), pltpu.VMEM(square, bf16),
        pltpu.VMEM(square, bf16), pltpu.VMEM(square, bf16),
        pltpu.VMEM((turns, rows_all, pos_pad), bf16),
        pltpu.VMEM((turns, n_blk, rows_blk, pos_pad), bf16),
        pltpu.VMEM((turns, rows_all, pos_pad), bf16),
        pltpu.VMEM((rows_all, pos_pad), bf16),
        pltpu.VMEM((ITERS, rows_all, filt), f32),
        pltpu.VMEM((ITERS, n_img, rows_img, filt), f32),
        pltpu.VMEM((rows_img, filt), f32),
        pltpu.VMEM((ITERS, rows_all, filt), f32),
        dma((n_img,)), dma((n_img,)), dma((n_img,)), dma((n_img,)),
        dma((turns, n_blk)), dma((turns, n_blk)), dma((turns, n_blk)), dma((turns, n_blk)),
        dma((ITERS, n_img)), dma((ITERS, n_img)), dma((ITERS, n_img)), dma((ITERS, n_img)),
    ]
    return kernel, scratch, scales


def round_up(value, unit):
    return -(-value // unit) * unit


def make_patches(images, pos_pad):
    count = images.shape[0]
    half = SIDE // 2
    pairs = images.reshape(count, SIDE, half, 2 * CHAN)
    pairs = jnp.pad(pairs, ((0, 0), (1, 1), (1, 0), (0, 0)))
    parts = []
    for row in range(3):
        lines = pairs[:, row:row + SIDE:2]
        parts += [lines[:, :, :half], lines[:, :, 1:]]
    patches = jnp.concatenate(parts, axis=-1).reshape(count * half * half, 12 * CHAN)
    return jnp.pad(patches, ((0, pos_pad - patches.shape[0]), (0, 0)))


def solution(mesh):
    n_img, n_blk = mesh.shape["img"], mesh.shape["blk"]

    def shards(images, filters, phases, labels, weights):
        filt, pos = filters.shape[0], labels.shape[0]
        pos_pad = round_up(pos, TILE)
        rows_img = round_up(LABELS, 8 * n_img) // n_img
        rows_blk = round_up(LABELS, 16 * n_blk) // n_blk
        rows_all = max(rows_img * n_img, rows_blk * n_blk)
        kernel, scratch, scales = make_kernel(
            n_img, n_blk, filt, pos, pos_pad, pos * n_img, rows_img, rows_blk, rows_all)
        patches = make_patches(images, pos_pad)
        taps = jnp.pad(filters.reshape(filt, 3, 3 * CHAN), ((0, 0), (0, 0), (CHAN, 0)))
        vmem = pl.BlockSpec(memory_space=pltpu.VMEM)
        return pl.pallas_call(
            kernel,
            out_shape=(jax.ShapeDtypeStruct((LABELS, filt), jnp.float32),
                       jax.ShapeDtypeStruct((LABELS, pos), jnp.float32)),
            in_specs=[vmem] * 5 + [pl.BlockSpec(memory_space=pltpu.SMEM)],
            out_specs=(vmem, vmem),
            scratch_shapes=scratch,
            compiler_params=pltpu.CompilerParams(
                collective_id=0, has_side_effects=True, vmem_limit_bytes=48 * 2**20),
        )(
            patches,
            taps.reshape(filt, 12 * CHAN),
            phases[:, None],
            jnp.pad(labels[None, :], ((0, 0), (0, pos_pad - pos)), constant_values=-1),
            jnp.pad(weights, ((0, rows_all - LABELS), (0, 0))),
            jnp.asarray(np.array(scales, np.float32)),
        )

    return jax.shard_map(
        shards,
        mesh=mesh,
        in_specs=(P("img", None, None), P("blk", None), P("blk"), P("img"), P(None, "blk")),
        out_specs=(P(None, "blk"), P(None, "img")),
        check_vma=False,
    )
```

time: 435 us -> 104 us (0.24); the launches traced: 429 us -> 104 us
  waiting for transfers between devices: 221 us -> 0 us
  other arithmetic: 130 us -> 0 us
  Pallas kernels: 0 us -> 96.8 us
  matrix products: 41.5 us -> 0 us
  between operations: 17.3 us -> 0.82 us
  local copies, waits for them, and re-layouts: 18.3 us -> 6.13 us
    psum x5 -> x0, waiting for transfers between devices: 221 us -> none  [the longest x2 115 us: shards(): projected = lax.psum(local_projection, 'img')]
    another operation x18 -> x0, other arithmetic: 119 us -> none  [the longest x14 78.8 us: shards(): factor = jnp.linalg.cholesky(gram)]
    pallas_call x0 -> x1, Pallas kernels: none -> 96.8 us  [shards(): pl.pallas_call(kernel, out_shape=(jax.ShapeDtypeStruct((LABELS, filt), jn...]
    another operation x34 -> x0, matrix products: 18 us -> none  [the longest x14 7.73 us: solve_with(): lax.linalg.triangular_solve(factor, projected, left_side=False, lower=Tru...]
    conv_general_dilated x1 -> x0, matrix products: 14.1 us -> none  [block_features(): lax.conv_general_dilated(pictures, kernel, (2, 2), ((1, 1), (1, 1)), dime...]
    another operation x34 -> x0, local copies, waits for them, and re-layouts: 12 us -> none  [the longest x21 11.3 us: solve_with(): lax.linalg.triangular_solve(factor, projected, left_side=False, lower=Tru...]
    dot_general x6 -> x0, matrix products: 9.36 us -> none  [the longest x2 4.02 us: shards(): lax.dot_general(residual.astype(jnp.bfloat16), features, (((1,), (1,)), (...]
    convert_element_type x1 -> x0, other arithmetic: 6.39 us -> none  [block_features(): (math.sqrt(2.0) * jnp.cos(response + phase_rows[:, None])).astype(jnp.bfl...]
  transfers between devices with their start and end apart: 5 -> 0, of which waited for: 5 -> 0; matrix products, arithmetic and copies ran while one was open for 0% -> 0% of each run, Pallas kernels for 0% -> 0%
where the time goes in v1:
time: 104 us
  Pallas kernels  96.8 us (93%)
  local copies, waits for them, and re-layouts  6.13 us (6%)
    pallas_call x1, Pallas kernels, shards(): pl.pallas_call(kernel, out_shape=(jax.ShapeDtypeStruct((LABELS, filt), jn...  96.8 us
    unnamed x17, local copies, waits for them, and re-layouts  3.45 us

profile of v1, /device:TPU:0, one launch (start us, length us, event | category | flops | bytes accessed | tf_op | source)
XLA Modules:
  0.0 103.7 jit_solution(11643203114843508716)
XLA Ops:
  0.6 1.3 %reshape.16 = bf16[4,28,14,128]{3,2,0,1:T(8,128)(2,1)S(1)} reshape(bf16[4,28,1792]{2,0,1:T(4,128)(2,1)} %param.6) | data formatting | bytes 802816 | tf_op jit(solution)/shard_map/reshape | solution.py:296
  1.9 0.2 pad_slice_fusion
  2.2 0.1 slice_dynamic-update-slice_fusion.4
  2.3 0.1 slice_dynamic-update-slice_fusion.3
  2.3 0.1 slice_dynamic-update-slice_fusion.2
  2.5 0.1 slice_dynamic-update-slice_fusion.1
  2.5 0.1 slice_dynamic-update-slice_fusion
  2.6 0.1 copy.10
  2.7 0.4 reshape.17
  3.1 0.0 copy-start.1
  3.1 0.1 pad.21.patches_ref
  3.2 1.0 copy-done.1
  4.2 0.1 pad.22
  4.3 0.0 copy-start.4
  4.3 0.0 copy-start.3
  4.3 0.0 copy-start
  4.3 0.3 copy.11.filters_ref
  4.6 0.6 copy-done.2
  5.2 0.1 copy.12.phases_ref
  5.4 0.0 copy-done.3
  5.4 0.0 copy-done
  5.4 96.8 %shard_map.77 = (f32[150,512]{1,0:T(8,128)S(1)}, f32[150,784]{1,0:T(8,128)S(1)}) custom-call(bf16[896,768]{1,0:T(8,128)(2,1)S(1)} %pad.21.patches_ref, bf16[512,768]{1,0:T(8,128)(2,1)S(1)} %copy.11.filters_ref, f32[512,1]{1,0:T(8,128)S(1)} %copy.12.phases_ref, s32[1,896]{1,0:T(1,128)S(1)} %pad.23.labels_ref, f32[192,512]{1,0:T(8,128)S(1)} %pad.24.weights_ref, ...), custom_call_target="tpu_custom_call" | custom-call | tf_op jit(solution)/shard_map/pallas_call | solution.py:320
  102.2 0.7 copy.20
  102.9 0.8 copy.21
  (6 shorter events, 0.1 us)
Async XLA Ops:
  3.1 1.1 %copy-start.1 = (bf16[512,576]{0,1:T(8,128)(2,1)S(1)}, bf16[512,576]{0,1:T(8,128)(2,1)}, u32[]{:S(2)}) copy-start(bf16[512,576]{0,1:T(8,128)(2,1)} %param.7) | copy-start | bytes 1769476
  4.2 1.0 copy-start.2
  4.3 0.9 copy-start.4
  4.3 1.1 %copy-start.3 = (s32[784]{0:T(1024)S(1)}, s32[784]{0:T(1024)}, u32[]{:S(2)}) copy-start(s32[784]{0:T(1024)} %param.9) | copy-start | bytes 9412
  4.3 1.1 %copy-start = (f32[9]{0:T(128)S(1)}, f32[9]{0:T(128)}, u32[]{:S(2)}) copy-start(f32[9]{0:T(128)} %constant.9.clone.scales_ref) | copy-start | bytes 112

commit v2 on v1

v2 whole, which is shorter than its diff:
```python
import math

import jax
import jax.numpy as jnp
import numpy as np
from jax import lax
from jax.experimental import pallas as pl
from jax.experimental.pallas import tpu as pltpu
from jax.sharding import PartitionSpec as P

SIDE = 28
CHAN = 64
LABELS = 150
ITERS = 2
RIDGE = 0.5
DAMPING = 0.75
TILE = 128


def cosine_coefficients(degree=6):
    nodes = np.cos((np.arange(400) + 0.5) * np.pi / 400)
    square = (nodes + 1.0) * (np.pi**2 * 1.0005) / 2
    fit = np.polynomial.chebyshev.Chebyshev.fit(square, np.sqrt(2.0) * np.cos(np.sqrt(square)), degree)
    return [float(c) for c in fit.convert(kind=np.polynomial.Polynomial).coef]


COEFFICIENTS = cosine_coefficients()
TURN_HIGH = 6.28125
TURN_LOW = 2.0 * math.pi - TURN_HIGH


def inverse_scales(lowest):
    scales = []
    while 1.0 - lowest > 1e-4:
        scale = 2.0 / (1.0 + lowest)
        scales.append(scale)
        lowest = scale * lowest * (2.0 - scale * lowest)
    return scales


def split(value):
    high = value.astype(jnp.bfloat16)
    return high, (value - high.astype(jnp.float32)).astype(jnp.bfloat16)


def dot(a, b):
    return jnp.dot(a, b, preferred_element_type=jnp.float32)


def dot_nt(a, b):
    return lax.dot_general(a, b, (((1,), (1,)), ((), ())), preferred_element_type=jnp.float32)


def dot_three(a_high, a_low, b_high, b_low):
    return dot(a_high, b_high) + (dot(a_high, b_low) + dot(a_low, b_high))


def make_groups(n_img, n_blk):
    unit = math.lcm(8 * n_img, 16 * n_blk)
    chunks = {"img": unit // n_img, "blk": unit // n_blk}
    last = math.lcm(*chunks.values())
    groups = []
    first = 0
    while first < LABELS:
        rows = min(unit, round_up(LABELS - first, last))
        groups.append((first, rows))
        first += rows
    return groups, chunks


def make_kernel(n_img, n_blk, filt, pos, pos_pad, pixels, groups, chunks):
    features_all = filt * n_blk
    shrink = 1.0 / math.sqrt(features_all)
    expand = math.sqrt(features_all)
    tiles = filt // TILE
    packed = tiles * (tiles + 1) // 2 * TILE
    rows_gram = packed // n_img
    rows_all = sum(rows for _, rows in groups)
    upper = (RIDGE + 2.0 * filt) * pixels
    scales = inverse_scales(RIDGE * pixels / upper)

    def kernel(
        patches_ref, filters_ref, phases_ref, labels_ref, weights_ref, scales_ref,
        out_weights, out_residual,
        feat, gram, gram_in, gram_all, h_high, h_low, x_high, x_low, y_high, y_low,
        part, part_in, part_all, proj, proj_in, w_all,
        gram_s, gram_r, gram_all_s, gram_all_r,
        part_s, part_r, part_all_s, part_all_r,
        proj_s, proj_r, w_s, w_r,
    ):
        place = {"img": lax.axis_index("img"), "blk": lax.axis_index("blk")}
        size = {"img": n_img, "blk": n_blk}
        barrier = pltpu.get_barrier_semaphore()

        def each_peer(axis, body, owners=None):
            me, n = place[axis], size[axis]
            stride = 1 if owners is None else n // owners

            def one(step, carry):
                peer = lax.rem(me + step, n)
                if owners is None or owners == n:
                    body(step, peer, peer)
                else:
                    @pl.when((lax.rem(peer, stride) == 0) & (peer < stride * owners))
                    def _():
                        body(step, peer, peer // stride)
                return carry

            lax.fori_loop(1, n, one, 0)

        def if_owner(axis, owners, body):
            me, n = place[axis], size[axis]
            stride = n // owners
            if owners == n:
                body(me)
            else:
                @pl.when((lax.rem(me, stride) == 0) & (me < stride * owners))
                def _():
                    body(me // stride)

        for axis in size:
            each_peer(axis, lambda step, peer, owner: pl.semaphore_signal(
                barrier, inc=1, device_id={axis: peer}, device_id_type=pl.DeviceIdType.MESH))

        unsent = []

        def span(first, owner, rows):
            return pl.ds(pl.multiple_of(first + owner * rows, 8), rows)

        def scatter(axis, first, rows, owners, source, target, send, recv):
            def copy(step, peer, owner, slot):
                return pltpu.make_async_remote_copy(
                    src_ref=source.at[span(first, owner, rows)],
                    dst_ref=target.at[slot],
                    send_sem=send.at[step], recv_sem=recv.at[slot],
                    device_id={axis: peer}, device_id_type=pl.DeviceIdType.MESH)

            def start():
                me = place[axis]
                each_peer(axis, lambda step, peer, owner: copy(step, peer, owner, me).start(), owners)

                def keep(owner):
                    target[me] = source[span(first, owner, rows), :]

                if_owner(axis, owners, keep)
                unsent.append(lambda: each_peer(
                    axis, lambda step, peer, owner: copy(step, peer, owner, me).wait_send(), owners))

            def wait():
                each_peer(axis, lambda step, peer, owner: copy(step, peer, 0, peer).wait_recv())

            return start, wait

        def gather(axis, first, rows, owners, whole, send, recv):
            def copy(step, peer, owner):
                at = whole.at[span(first, owner, rows)]
                return pltpu.make_async_remote_copy(
                    src_ref=at, dst_ref=at,
                    send_sem=send.at[step], recv_sem=recv.at[owner],
                    device_id={axis: peer}, device_id_type=pl.DeviceIdType.MESH)

            def start(value):
                def share(mine):
                    whole[span(first, mine, rows), :] = value(mine)
                    each_peer(axis, lambda step, peer, owner: copy(step, peer, mine).start())

                if_owner(axis, owners, share)
                unsent.append(lambda: if_owner(axis, owners, lambda mine: each_peer(
                    axis, lambda step, peer, owner: copy(step, peer, mine).wait_send())))

            def wait():
                each_peer(axis, lambda step, peer, owner: copy(step, peer, owner).wait_recv(), owners)

            return start, wait

        inside = lax.broadcasted_iota(jnp.int32, (TILE, pos_pad), 1) < pos
        for tile in range(tiles):
            here = slice(tile * TILE, (tile + 1) * TILE)
            angle = dot_nt(filters_ref[here, :], patches_ref[...]) + phases_ref[here, :]
            turns = jnp.floor(angle * (0.5 / math.pi) + 0.5)
            angle = (angle - turns * TURN_HIGH) - turns * TURN_LOW
            square = angle * angle
            value = jnp.full_like(square, COEFFICIENTS[-1])
            for coefficient in COEFFICIENTS[-2::-1]:
                value = value * square + coefficient
            feat[here, :] = jnp.where(inside, value, 0.0).astype(jnp.bfloat16)

        spot = 0
        for row in range(tiles):
            block = dot_nt(feat[row * TILE:(row + 1) * TILE, :], feat[: (row + 1) * TILE, :])
            for col in range(row + 1):
                gram[spot * TILE:(spot + 1) * TILE, :] = block[:, col * TILE:(col + 1) * TILE]
                spot += 1

        pl.semaphore_wait(barrier, n_img - 1 + n_blk - 1)
        gram_scatter = scatter("img", 0, rows_gram, n_img, gram, gram_in, gram_s, gram_r)
        gram_gather = gather("img", 0, rows_gram, n_img, gram_all, gram_all_s, gram_all_r)
        gram_scatter[0]()

        def transfers(axis, turn, g, source, target, whole, sems):
            first, rows = groups[g]
            chunk = chunks[axis]
            at = (turn, g)
            return (scatter(axis, first, chunk, rows // chunk, source.at[turn], target.at[at],
                            sems[0].at[at], sems[1].at[at])
                    + gather(axis, first, chunk, rows // chunk, whole.at[turn],
                             sems[2].at[at], sems[3].at[at]))

        def predict_transfers(turn, g):
            return transfers("blk", turn, g, part, part_in, part_all,
                             (part_s, part_r, part_all_s, part_all_r))

        def project_transfers(step, g):
            return transfers("img", step, g, proj, proj_in, w_all, (proj_s, proj_r, w_s, w_r))

        def rows_of(g):
            first, rows = groups[g]
            return slice(first, first + rows)

        def begin_predict(turn, g, weight_now):
            value = shrink * dot(weight_now.astype(jnp.bfloat16), feat[...])
            part[turn, rows_of(g), :] = value.astype(jnp.bfloat16)
            predict_transfers(turn, g)[0]()

        def middle_predict(turn, g):
            _, wait, share, _ = predict_transfers(turn, g)
            if_owner("blk", groups[g][1] // chunks["blk"], lambda mine: wait())
            share(lambda mine: jnp.sum(part_in[turn, g].astype(jnp.float32), axis=0).astype(jnp.bfloat16))

        def end_predict(turn, g):
            predict_transfers(turn, g)[3]()
            first, rows = groups[g]
            classes = lax.broadcasted_iota(jnp.int32, (rows, pos_pad), 0) + first
            targets = jnp.where(labels_ref[...] == classes, 1.0, 0.0)
            residual = targets - part_all[turn, rows_of(g), :].astype(jnp.float32)
            if turn < ITERS:
                proj[turn, rows_of(g), :] = dot_nt(residual.astype(jnp.bfloat16), feat[...])
                project_transfers(turn, g)[0]()
            else:
                end = min(first + rows, LABELS)
                out_residual[first:end, :] = residual[:end - first, :pos]

        def solve(step, g):
            _, wait, share, _ = project_transfers(step, g)

            def weight_next(mine):
                here = span(groups[g][0], mine, chunks["img"])
                before = weights_ref[here, :] if step == 0 else w_all[step - 1, here, :]
                p_high, p_low = split(jnp.sum(proj_in[step, g], axis=0))
                change = expand * dot_three(p_high, p_low, x_high[...], x_low[...])
                return before + DAMPING * change

            if_owner("img", groups[g][1] // chunks["img"], lambda mine: wait())
            share(weight_next)

        def use_weights(step, g):
            project_transfers(step, g)[3]()
            begin_predict(step + 1, g, w_all[step, rows_of(g), :])
            if step == ITERS - 1:
                first, rows = groups[g]
                end = min(first + rows, LABELS)
                out_weights[first:end, :] = w_all[step, first:end, :]

        every = range(len(groups))
        for g in every:
            begin_predict(0, g, weights_ref[rows_of(g), :])
        gram_scatter[1]()
        gram_gather[0](lambda mine: jnp.sum(gram_in[...], axis=0))
        for g in every:
            middle_predict(0, g)
        gram_gather[1]()

        spot = 0
        diagonal = (lax.broadcasted_iota(jnp.int32, (TILE, TILE), 0)
                    == lax.broadcasted_iota(jnp.int32, (TILE, TILE), 1))
        scale = scales[0]
        for row in range(tiles):
            for col in range(row + 1):
                block = gram_all[spot * TILE:(spot + 1) * TILE, :]
                spot += 1
                if row == col:
                    block = block + jnp.where(diagonal, RIDGE * pixels, 0.0)
                start = block * (-scale * scale / upper / upper)
                if row == col:
                    start = start + jnp.where(diagonal, 2.0 * scale / upper, 0.0)
                places = [(row, col, block, start)]
                if row != col:
                    places.append((col, row, block.T, start.T))
                for down, across, h_part, x_part in places:
                    at = (slice(down * TILE, (down + 1) * TILE), slice(across * TILE, (across + 1) * TILE))
                    h_high[at], h_low[at] = split(h_part)
                    x_high[at], x_low[at] = split(x_part)

        for g in every:
            end_predict(0, g)

        def newton(step, carry):
            scale = scales_ref[step]
            y = dot_three(h_high[...], h_low[...], x_high[...], x_low[...]) * (-scale)
            same = (lax.broadcasted_iota(jnp.int32, (filt, filt), 0)
                    == lax.broadcasted_iota(jnp.int32, (filt, filt), 1))
            y_high[...], y_low[...] = split(y + jnp.where(same, 2.0, 0.0))
            x = dot_three(x_high[...], x_low[...], y_high[...], y_low[...]) * scale
            x_high[...], x_low[...] = split(x)
            return carry

        lax.fori_loop(1, len(scales), newton, 0)

        stages = []
        for step in range(ITERS):
            stages += [
                lambda g, step=step: solve(step, g),
                lambda g, step=step: use_weights(step, g),
                lambda g, step=step: middle_predict(step + 1, g),
                lambda g, step=step: end_predict(step + 1, g),
            ]
        for tick in range(len(stages) + len(groups) - 1):
            for g in every:
                if 0 <= tick - g < len(stages):
                    stages[tick - g](g)
        for wait_sent in unsent:
            wait_sent()

    f32, bf16 = jnp.float32, jnp.bfloat16
    square = (filt, filt)
    dma = pltpu.SemaphoreType.DMA
    turns, count = ITERS + 1, len(groups)
    scratch = [
        pltpu.VMEM((filt, pos_pad), bf16),
        pltpu.VMEM((packed, TILE), f32),
        pltpu.VMEM((n_img, rows_gram, TILE), f32),
        pltpu.VMEM((packed, TILE), f32),
        pltpu.VMEM(square, bf16), pltpu.VMEM(square, bf16),
        pltpu.VMEM(square, bf16), pltpu.VMEM(square, bf16),
        pltpu.VMEM(square, bf16), pltpu.VMEM(square, bf16),
        pltpu.VMEM((turns, rows_all, pos_pad), bf16),
        pltpu.VMEM((turns, count, n_blk, chunks["blk"], pos_pad), bf16),
        pltpu.VMEM((turns, rows_all, pos_pad), bf16),
        pltpu.VMEM((ITERS, rows_all, filt), f32),
        pltpu.VMEM((ITERS, count, n_img, chunks["img"], filt), f32),
        pltpu.VMEM((ITERS, rows_all, filt), f32),
        dma((n_img,)), dma((n_img,)), dma((n_img,)), dma((n_img,)),
    ]
    scratch += [dma((turns, count, n_blk))] * 4 + [dma((ITERS, count, n_img))] * 4
    return kernel, scratch, scales, rows_all


def round_up(value, unit):
    return -(-value // unit) * unit


def make_patches(images, pos_pad):
    count = images.shape[0]
    half = SIDE // 2
    pairs = images.reshape(count, SIDE, half, 2 * CHAN)
    pairs = jnp.pad(pairs, ((0, 0), (1, 1), (1, 0), (0, 0)))
    parts = []
    for row in range(3):
        lines = pairs[:, row:row + SIDE:2]
        parts += [lines[:, :, :half], lines[:, :, 1:]]
    patches = jnp.concatenate(parts, axis=-1).reshape(count * half * half, 12 * CHAN)
    return jnp.pad(patches, ((0, pos_pad - patches.shape[0]), (0, 0)))


def solution(mesh):
    n_img, n_blk = mesh.shape["img"], mesh.shape["blk"]

    def shards(images, filters, phases, labels, weights):
        filt, pos = filters.shape[0], labels.shape[0]
        pos_pad = round_up(pos, TILE)
        groups, chunks = make_groups(n_img, n_blk)
        kernel, scratch, scales, rows_all = make_kernel(
            n_img, n_blk, filt, pos, pos_pad, pos * n_img, groups, chunks)
        patches = make_patches(images, pos_pad)
        taps = jnp.pad(filters.reshape(filt, 3, 3 * CHAN), ((0, 0), (0, 0), (CHAN, 0)))
        vmem = pl.BlockSpec(memory_space=pltpu.VMEM)
        return pl.pallas_call(
            kernel,
            out_shape=(jax.ShapeDtypeStruct((LABELS, filt), jnp.float32),
                       jax.ShapeDtypeStruct((LABELS, pos), jnp.float32)),
            in_specs=[vmem] * 5 + [pl.BlockSpec(memory_space=pltpu.SMEM)],
            out_specs=(vmem, vmem),
            scratch_shapes=scratch,
            compiler_params=pltpu.CompilerParams(
                collective_id=0, has_side_effects=True, vmem_limit_bytes=48 * 2**20),
        )(
            patches,
            taps.reshape(filt, 12 * CHAN),
            phases[:, None],
            jnp.pad(labels[None, :], ((0, 0), (0, pos_pad - pos)), constant_values=-1),
            jnp.pad(weights, ((0, rows_all - LABELS), (0, 0))),
            jnp.asarray(np.array(scales, np.float32)),
        )

    return jax.shard_map(
        shards,
        mesh=mesh,
        in_specs=(P("img", None, None), P("blk", None), P("blk"), P("img"), P(None, "blk")),
        out_specs=(P(None, "blk"), P(None, "img")),
        check_vma=False,
    )
```

time: 104 us -> 91.8 us (0.88)
  Pallas kernels: 96.8 us -> 84.7 us
    pallas_call x1, Pallas kernels: 96.8 us -> 84.7 us  [shards(): pl.pallas_call(kernel, out_shape=(jax.ShapeDtypeStruct((LABELS, filt), jn...]
where the time goes in v2:
time: 91.8 us; the launch traced here: 91.6 us
  Pallas kernels  84.7 us (92%)
  local copies, waits for them, and re-layouts  6.12 us (7%)
    pallas_call x1, Pallas kernels, shards(): pl.pallas_call(kernel, out_shape=(jax.ShapeDtypeStruct((LABELS, filt), jn...  84.7 us
    unnamed x17, local copies, waits for them, and re-layouts  3.45 us

profile of v2, /device:TPU:0, one launch (start us, length us, event | category | flops | bytes accessed | tf_op | source)
XLA Modules:
  0.0 91.6 jit_solution(8651995908086835780)
XLA Ops:
  0.6 1.3 %reshape.16 = bf16[4,28,14,128]{3,2,0,1:T(8,128)(2,1)S(1)} reshape(bf16[4,28,1792]{2,0,1:T(4,128)(2,1)} %param.6) | data formatting | bytes 802816 | tf_op jit(solution)/shard_map/reshape | solution.py:355
  1.9 0.2 pad_slice_fusion
  2.2 0.1 slice_dynamic-update-slice_fusion.4
  2.3 0.1 slice_dynamic-update-slice_fusion.3
  2.3 0.1 slice_dynamic-update-slice_fusion.2
  2.5 0.1 slice_dynamic-update-slice_fusion.1
  2.5 0.1 slice_dynamic-update-slice_fusion
  2.6 0.1 copy.10
  2.7 0.4 reshape.17
  3.1 0.0 copy-start.1
  3.1 0.1 pad.21.patches_ref
  3.2 1.0 %copy-done.1 = bf16[512,576]{0,1:T(8,128)(2,1)S(1)} copy-done((bf16[512,576]{0,1:T(8,128)(2,1)S(1)}, bf16[512,576]{0,1:T(8,128)(2,1)}, u32[]{:S(2)}) %copy-start.1) | copy-done | bytes 589848
  4.2 0.1 pad.22
  4.3 0.0 copy-start.4
  4.3 0.0 copy-start.3
  4.3 0.0 copy-start
  4.3 0.3 copy.11.filters_ref
  4.6 0.6 copy-done.2
  5.2 0.0 copy-done.4
  5.2 0.1 copy.12.phases_ref
  5.4 0.0 copy-done.3
  5.4 84.7 %shard_map.77 = (f32[150,512]{1,0:T(8,128)S(1)}, f32[150,784]{1,0:T(8,128)S(1)}) custom-call(bf16[896,768]{1,0:T(8,128)(2,1)S(1)} %pad.21.patches_ref, bf16[512,768]{1,0:T(8,128)(2,1)S(1)} %copy.11.filters_ref, f32[512,1]{1,0:T(8,128)S(1)} %copy.12.phases_ref, s32[1,896]{1,0:T(1,128)S(1)} %pad.23.labels_ref, f32[160,512]{1,0:T(8,128)S(1)} %pad.24.weights_ref, ...), custom_call_target="tpu_custom_call" | custom-call | tf_op jit(solution)/shard_map/pallas_call | solution.py:377
  90.1 0.7 copy.20
  90.8 0.8 copy.21
  (6 shorter events, 0.1 us)
Async XLA Ops:
  3.1 1.1 %copy-start.1 = (bf16[512,576]{0,1:T(8,128)(2,1)S(1)}, bf16[512,576]{0,1:T(8,128)(2,1)}, u32[]{:S(2)}) copy-start(bf16[512,576]{0,1:T(8,128)(2,1)} %param.7) | copy-start | bytes 1769476
  4.2 1.0 %copy-start.2 = (f32[150,512]{1,0:T(8,128)S(1)}, f32[150,512]{1,0:T(8,128)}, u32[]{:S(2)}) copy-start(f32[150,512]{1,0:T(8,128)} %param.10) | copy-start | bytes 921604
  4.3 0.9 %copy-start.4 = (f32[512]{0:T(512)S(1)}, f32[512]{0:T(512)}, u32[]{:S(2)}) copy-start(f32[512]{0:T(512)} %param.8) | copy-start | bytes 6148
  4.3 1.1 %copy-start.3 = (s32[784]{0:T(1024)S(1)}, s32[784]{0:T(1024)}, u32[]{:S(2)}) copy-start(s32[784]{0:T(1024)} %param.9) | copy-start | bytes 9412
  4.3 1.1 %copy-start = (f32[8]{0:T(128)S(1)}, f32[8]{0:T(128)}, u32[]{:S(2)}) copy-start(f32[8]{0:T(128)} %constant.9.clone.scales_ref) | copy-start | bytes 100

commit v3 on v2

--- a/solution.py
+++ b/solution.py
@@ -15,6 +15,7 @@
 RIDGE = 0.5
 DAMPING = 0.75
 TILE = 128
+PANEL = 256
 
 
 def cosine_coefficients(degree=6):
@@ -52,7 +53,7 @@
 
 
 def dot_three(a_high, a_low, b_high, b_low):
-    return dot(a_high, b_high) + (dot(a_high, b_low) + dot(a_low, b_high))
+    return dot(jnp.concatenate([a_high, a_high, a_low], 1), jnp.concatenate([b_high, b_low, b_high], 0))
 
 
 def make_groups(n_img, n_blk):
@@ -173,24 +174,30 @@
 
             return start, wait
 
-        inside = lax.broadcasted_iota(jnp.int32, (TILE, pos_pad), 1) < pos
-        for tile in range(tiles):
-            here = slice(tile * TILE, (tile + 1) * TILE)
-            angle = dot_nt(filters_ref[here, :], patches_ref[...]) + phases_ref[here, :]
+        for left in range(0, pos_pad, PANEL):
+            here = slice(left, min(left + PANEL, pos_pad))
+            angle = dot_nt(filters_ref[...], patches_ref[here, :]) + phases_ref[...]
             turns = jnp.floor(angle * (0.5 / math.pi) + 0.5)
             angle = (angle - turns * TURN_HIGH) - turns * TURN_LOW
             square = angle * angle
             value = jnp.full_like(square, COEFFICIENTS[-1])
             for coefficient in COEFFICIENTS[-2::-1]:
                 value = value * square + coefficient
-            feat[here, :] = jnp.where(inside, value, 0.0).astype(jnp.bfloat16)
-
-        spot = 0
-        for row in range(tiles):
-            block = dot_nt(feat[row * TILE:(row + 1) * TILE, :], feat[: (row + 1) * TILE, :])
-            for col in range(row + 1):
-                gram[spot * TILE:(spot + 1) * TILE, :] = block[:, col * TILE:(col + 1) * TILE]
-                spot += 1
+            if here.stop > pos:
+                inside = lax.broadcasted_iota(jnp.int32, value.shape, 1) < pos - left
+                value = jnp.where(inside, value, 0.0)
+            feat[:, here] = value.astype(jnp.bfloat16)
+
+        def spot_of(row, col):
+            return slice((row * (row + 1) // 2 + col) * TILE, (row * (row + 1) // 2 + col + 1) * TILE)
+
+        for left in range(0, filt, PANEL):
+            block = dot_nt(feat[left:, :], feat[left:left + PANEL, :])
+            for row in range(left // TILE, tiles):
+                for col in range(left // TILE, min(left + PANEL, filt) // TILE):
+                    if col <= row:
+                        gram[spot_of(row, col), :] = block[
+                            row * TILE - left:(row + 1) * TILE - left, col * TILE - left:(col + 1) * TILE - left]
 
         pl.semaphore_wait(barrier, n_img - 1 + n_blk - 1)
         gram_scatter = scatter("img", 0, rows_gram, n_img, gram, gram_in, gram_s, gram_r)
@@ -246,9 +253,14 @@
             def weight_next(mine):
                 here = span(groups[g][0], mine, chunks["img"])
                 before = weights_ref[here, :] if step == 0 else w_all[step - 1, here, :]
-                p_high, p_low = split(jnp.sum(proj_in[step, g], axis=0))
-                change = expand * dot_three(p_high, p_low, x_high[...], x_low[...])
-                return before + DAMPING * change
+                total = jnp.sum(proj_in[step, g], axis=0)
+                p_high = total.astype(jnp.bfloat16)
+                high = p_high.astype(jnp.float32)
+                both = jnp.concatenate([high, total - high], 0).astype(jnp.bfloat16)
+                change = dot(both, x_high[last])
+                rows = total.shape[0]
+                change = change[:rows] + (change[rows:] + dot(p_high, x_low[last]))
+                return before + DAMPING * (expand * change)
 
             if_owner("img", groups[g][1] // chunks["img"], lambda mine: wait())
             share(weight_next)
@@ -270,14 +282,12 @@
             middle_predict(0, g)
         gram_gather[1]()
 
-        spot = 0
         diagonal = (lax.broadcasted_iota(jnp.int32, (TILE, TILE), 0)
                     == lax.broadcasted_iota(jnp.int32, (TILE, TILE), 1))
         scale = scales[0]
         for row in range(tiles):
             for col in range(row + 1):
-                block = gram_all[spot * TILE:(spot + 1) * TILE, :]
-                spot += 1
+                block = gram_all[spot_of(row, col), :]
                 if row == col:
                     block = block + jnp.where(diagonal, RIDGE * pixels, 0.0)
                 start = block * (-scale * scale / upper / upper)
@@ -289,22 +299,28 @@
                 for down, across, h_part, x_part in places:
                     at = (slice(down * TILE, (down + 1) * TILE), slice(across * TILE, (across + 1) * TILE))
                     h_high[at], h_low[at] = split(h_part)
+                    at = (1,) + at
                     x_high[at], x_low[at] = split(x_part)
+
+        def newton(step, carry):
+            scale = scales_ref[step]
+            now, later = lax.rem(step, 2), lax.rem(step + 1, 2)
+            for left in range(0, filt, PANEL):
+                here = slice(left, left + PANEL)
+                y = dot_three(h_high[...], h_low[...], x_high[now, :, here], x_low[now, :, here])
+                same = (lax.broadcasted_iota(jnp.int32, y.shape, 0)
+                        == lax.broadcasted_iota(jnp.int32, y.shape, 1) + left)
+                y_high[:, here], y_low[:, here] = split(jnp.where(same, 2.0, 0.0) - scale * y)
+            for left in range(0, filt, PANEL):
+                here = slice(left, left + PANEL)
+                x = dot_three(x_high[now], x_low[now], y_high[:, here], y_low[:, here])
+                x_high[later, :, here], x_low[later, :, here] = split(scale * x)
+            return carry
 
         for g in every:
             end_predict(0, g)
-
-        def newton(step, carry):
-            scale = scales_ref[step]
-            y = dot_three(h_high[...], h_low[...], x_high[...], x_low[...]) * (-scale)
-            same = (lax.broadcasted_iota(jnp.int32, (filt, filt), 0)
-                    == lax.broadcasted_iota(jnp.int32, (filt, filt), 1))
-            y_high[...], y_low[...] = split(y + jnp.where(same, 2.0, 0.0))
-            x = dot_three(x_high[...], x_low[...], y_high[...], y_low[...]) * scale
-            x_high[...], x_low[...] = split(x)
-            return carry
-
         lax.fori_loop(1, len(scales), newton, 0)
+        last = len(scales) % 2
 
         stages = []
         for step in range(ITERS):
@@ -331,7 +347,7 @@
         pltpu.VMEM((n_img, rows_gram, TILE), f32),
         pltpu.VMEM((packed, TILE), f32),
         pltpu.VMEM(square, bf16), pltpu.VMEM(square, bf16),
-        pltpu.VMEM(square, bf16), pltpu.VMEM(square, bf16),
+        pltpu.VMEM((2,) + square, bf16), pltpu.VMEM((2,) + square, bf16),
         pltpu.VMEM(square, bf16), pltpu.VMEM(square, bf16),
         pltpu.VMEM((turns, rows_all, pos_pad), bf16),
         pltpu.VMEM((turns, count, n_blk, chunks["blk"], pos_pad), bf16),

time: 91.8 us -> 97.5 us (1.062)
  Pallas kernels: 84.7 us -> 90.3 us
    pallas_call x1, Pallas kernels: 84.7 us -> 90.3 us  [shards(): pl.pallas_call(kernel, out_shape=(jax.ShapeDtypeStruct((LABELS, filt), jn...]
where the time goes in v3:
time: 97.5 us; the launch traced here: 97.3 us
  Pallas kernels  90.3 us (93%)
  local copies, waits for them, and re-layouts  6.12 us (6%)
    pallas_call x1, Pallas kernels, shards(): pl.pallas_call(kernel, out_shape=(jax.ShapeDtypeStruct((LABELS, filt), jn...  90.3 us
    unnamed x17, local copies, waits for them, and re-layouts  3.45 us

profile of v3, /device:TPU:0, one launch (start us, length us, event | category | flops | bytes accessed | tf_op | source)
XLA Modules:
  0.0 97.3 jit_solution(12380301359953626149)
XLA Ops:
  0.6 1.3 %reshape.16 = bf16[4,28,14,128]{3,2,0,1:T(8,128)(2,1)S(1)} reshape(bf16[4,28,1792]{2,0,1:T(4,128)(2,1)} %param.6) | data formatting | bytes 802816 | tf_op jit(solution)/shard_map/reshape | solution.py:371
  1.9 0.2 pad_slice_fusion
  2.2 0.1 slice_dynamic-update-slice_fusion.4
  2.3 0.1 slice_dynamic-update-slice_fusion.3
  2.3 0.1 slice_dynamic-update-slice_fusion.2
  2.5 0.1 slice_dynamic-update-slice_fusion.1
  2.5 0.1 slice_dynamic-update-slice_fusion
  2.6 0.1 copy.10
  2.7 0.4 reshape.17
  3.1 0.0 copy-start.1
  3.1 0.1 pad.21.patches_ref
  3.2 1.0 copy-done.1
  4.2 0.1 pad.22
  4.3 0.0 copy-start.4
  4.3 0.0 copy-start.3
  4.3 0.0 copy-start
  4.3 0.3 copy.11.filters_ref
  4.6 0.6 copy-done.2
  5.2 0.0 copy-done.4
  5.2 0.1 copy.12.phases_ref
  5.4 0.0 copy-done.3
  5.4 90.3 %shard_map.77 = (f32[150,512]{1,0:T(8,128)S(1)}, f32[150,784]{1,0:T(8,128)S(1)}) custom-call(bf16[896,768]{1,0:T(8,128)(2,1)S(1)} %pad.21.patches_ref, bf16[512,768]{1,0:T(8,128)(2,1)S(1)} %copy.11.filters_ref, f32[512,1]{1,0:T(8,128)S(1)} %copy.12.phases_ref, s32[1,896]{1,0:T(1,128)S(1)} %pad.23.labels_ref, f32[160,512]{1,0:T(8,128)S(1)} %pad.24.weights_ref, ...), custom_call_target="tpu_custom_call" | custom-call | tf_op jit(solution)/shard_map/pallas_call | solution.py:393
  95.7 0.7 copy.20
  96.5 0.8 copy.21
  (6 shorter events, 0.1 us)
Async XLA Ops:
  3.1 1.1 %copy-start.1 = (bf16[512,576]{0,1:T(8,128)(2,1)S(1)}, bf16[512,576]{0,1:T(8,128)(2,1)}, u32[]{:S(2)}) copy-start(bf16[512,576]{0,1:T(8,128)(2,1)} %param.7) | copy-start | bytes 1769476
  4.2 1.0 copy-start.2
  4.3 0.9 copy-start.4
  4.3 1.1 %copy-start.3 = (s32[784]{0:T(1024)S(1)}, s32[784]{0:T(1024)}, u32[]{:S(2)}) copy-start(s32[784]{0:T(1024)} %param.9) | copy-start | bytes 9412
  4.3 1.1 %copy-start = (f32[8]{0:T(128)S(1)}, f32[8]{0:T(128)}, u32[]{:S(2)}) copy-start(f32[8]{0:T(128)} %constant.9.clone.scales_ref) | copy-start | bytes 100

commit v4 on v3

--- a/solution.py
+++ b/solution.py
@@ -174,30 +174,27 @@
 
             return start, wait
 
-        for left in range(0, pos_pad, PANEL):
-            here = slice(left, min(left + PANEL, pos_pad))
-            angle = dot_nt(filters_ref[...], patches_ref[here, :]) + phases_ref[...]
+        for top in range(0, filt, PANEL):
+            here = slice(top, top + PANEL)
+            angle = dot_nt(filters_ref[here, :], patches_ref[...]) + phases_ref[here, :]
             turns = jnp.floor(angle * (0.5 / math.pi) + 0.5)
             angle = (angle - turns * TURN_HIGH) - turns * TURN_LOW
             square = angle * angle
             value = jnp.full_like(square, COEFFICIENTS[-1])
             for coefficient in COEFFICIENTS[-2::-1]:
                 value = value * square + coefficient
-            if here.stop > pos:
-                inside = lax.broadcasted_iota(jnp.int32, value.shape, 1) < pos - left
-                value = jnp.where(inside, value, 0.0)
-            feat[:, here] = value.astype(jnp.bfloat16)
+            inside = lax.broadcasted_iota(jnp.int32, value.shape, 1) < pos
+            feat[here, :] = jnp.where(inside, value, 0.0).astype(jnp.bfloat16)
 
         def spot_of(row, col):
             return slice((row * (row + 1) // 2 + col) * TILE, (row * (row + 1) // 2 + col + 1) * TILE)
 
-        for left in range(0, filt, PANEL):
-            block = dot_nt(feat[left:, :], feat[left:left + PANEL, :])
-            for row in range(left // TILE, tiles):
-                for col in range(left // TILE, min(left + PANEL, filt) // TILE):
-                    if col <= row:
-                        gram[spot_of(row, col), :] = block[
-                            row * TILE - left:(row + 1) * TILE - left, col * TILE - left:(col + 1) * TILE - left]
+        for top in range(0, filt, PANEL):
+            block = dot_nt(feat[top:top + PANEL, :], feat[:top + PANEL, :])
+            for row in range(top // TILE, (top + PANEL) // TILE):
+                for col in range(row + 1):
+                    gram[spot_of(row, col), :] = block[
+                        row * TILE - top:(row + 1) * TILE - top, col * TILE:(col + 1) * TILE]
 
         pl.semaphore_wait(barrier, n_img - 1 + n_blk - 1)
         gram_scatter = scatter("img", 0, rows_gram, n_img, gram, gram_in, gram_s, gram_r)
@@ -257,9 +254,9 @@
                 p_high = total.astype(jnp.bfloat16)
                 high = p_high.astype(jnp.float32)
                 both = jnp.concatenate([high, total - high], 0).astype(jnp.bfloat16)
-                change = dot(both, x_high[last])
+                change = dot(both, x_high[...])
                 rows = total.shape[0]
-                change = change[:rows] + (change[rows:] + dot(p_high, x_low[last]))
+                change = change[:rows] + (change[rows:] + dot(p_high, x_low[...]))
                 return before + DAMPING * (expand * change)
 
             if_owner("img", groups[g][1] // chunks["img"], lambda mine: wait())
@@ -299,28 +296,25 @@
                 for down, across, h_part, x_part in places:
                     at = (slice(down * TILE, (down + 1) * TILE), slice(across * TILE, (across + 1) * TILE))
                     h_high[at], h_low[at] = split(h_part)
-                    at = (1,) + at
                     x_high[at], x_low[at] = split(x_part)
 
         def newton(step, carry):
             scale = scales_ref[step]
-            now, later = lax.rem(step, 2), lax.rem(step + 1, 2)
-            for left in range(0, filt, PANEL):
-                here = slice(left, left + PANEL)
-                y = dot_three(h_high[...], h_low[...], x_high[now, :, here], x_low[now, :, here])
-                same = (lax.broadcasted_iota(jnp.int32, y.shape, 0)
-                        == lax.broadcasted_iota(jnp.int32, y.shape, 1) + left)
-                y_high[:, here], y_low[:, here] = split(jnp.where(same, 2.0, 0.0) - scale * y)
-            for left in range(0, filt, PANEL):
-                here = slice(left, left + PANEL)
-                x = dot_three(x_high[now], x_low[now], y_high[:, here], y_low[:, here])
-                x_high[later, :, here], x_low[later, :, here] = split(scale * x)
+            for top in range(0, filt, PANEL):
+                here = slice(top, top + PANEL)
+                y = dot_three(h_high[here, :], h_low[here, :], x_high[...], x_low[...])
+                same = (lax.broadcasted_iota(jnp.int32, y.shape, 0) + top
+                        == lax.broadcasted_iota(jnp.int32, y.shape, 1))
+                y_high[here, :], y_low[here, :] = split(jnp.where(same, 2.0, 0.0) - scale * y)
+            for top in range(0, filt, PANEL):
+                here = slice(top, top + PANEL)
+                x = dot_three(x_high[here, :], x_low[here, :], y_high[...], y_low[...])
+                x_high[here, :], x_low[here, :] = split(scale * x)
             return carry
 
         for g in every:
             end_predict(0, g)
         lax.fori_loop(1, len(scales), newton, 0)
-        last = len(scales) % 2
 
         stages = []
         for step in range(ITERS):
@@ -347,7 +341,7 @@
         pltpu.VMEM((n_img, rows_gram, TILE), f32),
         pltpu.VMEM((packed, TILE), f32),
         pltpu.VMEM(square, bf16), pltpu.VMEM(square, bf16),
-        pltpu.VMEM((2,) + square, bf16), pltpu.VMEM((2,) + square, bf16),
+        pltpu.VMEM(square, bf16), pltpu.VMEM(square, bf16),
         pltpu.VMEM(square, bf16), pltpu.VMEM(square, bf16),
         pltpu.VMEM((turns, rows_all, pos_pad), bf16),
         pltpu.VMEM((turns, count, n_blk, chunks["blk"], pos_pad), bf16),

time: 97.5 us -> 92.3 us (0.947)
  Pallas kernels: 90.3 us -> 85.2 us
    pallas_call x1, Pallas kernels: 90.3 us -> 85.2 us  [shards(): pl.pallas_call(kernel, out_shape=(jax.ShapeDtypeStruct((LABELS, filt), jn...]
where the time goes in v4:
time: 92.3 us; the launch traced here: 92.1 us
  Pallas kernels  85.2 us (92%)
  local copies, waits for them, and re-layouts  6.12 us (7%)
    pallas_call x1, Pallas kernels, shards(): pl.pallas_call(kernel, out_shape=(jax.ShapeDtypeStruct((LABELS, filt), jn...  85.2 us
    unnamed x17, local copies, waits for them, and re-layouts  3.45 us

profile of v4, /device:TPU:0, one launch (start us, length us, event | category | flops | bytes accessed | tf_op | source)
XLA Modules:
  0.0 92.1 jit_solution(13496243352584109833)
XLA Ops:
  0.6 1.3 %reshape.16 = bf16[4,28,14,128]{3,2,0,1:T(8,128)(2,1)S(1)} reshape(bf16[4,28,1792]{2,0,1:T(4,128)(2,1)} %param.6) | data formatting | bytes 802816 | tf_op jit(solution)/shard_map/reshape | solution.py:365
  1.9 0.2 pad_slice_fusion
  2.2 0.1 slice_dynamic-update-slice_fusion.4
  2.3 0.1 slice_dynamic-update-slice_fusion.3
  2.3 0.1 slice_dynamic-update-slice_fusion.2
  2.5 0.1 slice_dynamic-update-slice_fusion.1
  2.5 0.1 slice_dynamic-update-slice_fusion
  2.6 0.1 copy.10
  2.7 0.4 reshape.17
  3.1 0.0 copy-start.1
  3.1 0.1 pad.21.patches_ref
  3.2 1.0 %copy-done.1 = bf16[512,576]{0,1:T(8,128)(2,1)S(1)} copy-done((bf16[512,576]{0,1:T(8,128)(2,1)S(1)}, bf16[512,576]{0,1:T(8,128)(2,1)}, u32[]{:S(2)}) %copy-start.1) | copy-done | bytes 589848
  4.2 0.1 pad.22
  4.3 0.0 copy-start.4
  4.3 0.0 copy-start.3
  4.3 0.0 copy-start
  4.3 0.3 copy.11.filters_ref
  4.6 0.6 copy-done.2
  5.2 0.0 copy-done.4
  5.2 0.1 copy.12.phases_ref
  5.4 0.0 copy-done
  5.4 85.2 %shard_map.77 = (f32[150,512]{1,0:T(8,128)S(1)}, f32[150,784]{1,0:T(8,128)S(1)}) custom-call(bf16[896,768]{1,0:T(8,128)(2,1)S(1)} %pad.21.patches_ref, bf16[512,768]{1,0:T(8,128)(2,1)S(1)} %copy.11.filters_ref, f32[512,1]{1,0:T(8,128)S(1)} %copy.12.phases_ref, s32[1,896]{1,0:T(1,128)S(1)} %pad.23.labels_ref, f32[160,512]{1,0:T(8,128)S(1)} %pad.24.weights_ref, ...), custom_call_target="tpu_custom_call" | custom-call | tf_op jit(solution)/shard_map/pallas_call | solution.py:387
  90.6 0.7 copy.20
  91.3 0.8 copy.21
  (6 shorter events, 0.1 us)
Async XLA Ops:
  3.1 1.1 %copy-start.1 = (bf16[512,576]{0,1:T(8,128)(2,1)S(1)}, bf16[512,576]{0,1:T(8,128)(2,1)}, u32[]{:S(2)}) copy-start(bf16[512,576]{0,1:T(8,128)(2,1)} %param.7) | copy-start | bytes 1769476
  4.2 1.0 %copy-start.2 = (f32[150,512]{1,0:T(8,128)S(1)}, f32[150,512]{1,0:T(8,128)}, u32[]{:S(2)}) copy-start(f32[150,512]{1,0:T(8,128)} %param.10) | copy-start | bytes 921604
  4.3 0.9 %copy-start.4 = (f32[512]{0:T(512)S(1)}, f32[512]{0:T(512)}, u32[]{:S(2)}) copy-start(f32[512]{0:T(512)} %param.8) | copy-start | bytes 6148
  4.3 1.1 %copy-start.3 = (s32[784]{0:T(1024)S(1)}, s32[784]{0:T(1024)}, u32[]{:S(2)}) copy-start(s32[784]{0:T(1024)} %param.9) | copy-start | bytes 9412
  4.3 1.1 %copy-start = (f32[8]{0:T(128)S(1)}, f32[8]{0:T(128)}, u32[]{:S(2)}) copy-start(f32[8]{0:T(128)} %constant.9.clone.scales_ref) | copy-start | bytes 100

commit v5 on v4

--- a/solution.py
+++ b/solution.py
@@ -75,7 +75,9 @@
     expand = math.sqrt(features_all)
     tiles = filt // TILE
     packed = tiles * (tiles + 1) // 2 * TILE
+    half = packed // 2
     rows_gram = packed // n_img
+    pairs = n_img // 2
     rows_all = sum(rows for _, rows in groups)
     upper = (RIDGE + 2.0 * filt) * pixels
     scales = inverse_scales(RIDGE * pixels / upper)
@@ -83,7 +85,7 @@
     def kernel(
         patches_ref, filters_ref, phases_ref, labels_ref, weights_ref, scales_ref,
         out_weights, out_residual,
-        feat, gram, gram_in, gram_all, h_high, h_low, x_high, x_low, y_high, y_low,
+        feat, gram, gram_half, gram_sum, gram_in, gram_all, h_high, h_low, x_high, x_low, y_high, y_low,
         part, part_in, part_all, proj, proj_in, w_all,
         gram_s, gram_r, gram_all_s, gram_all_r,
         part_s, part_r, part_all_s, part_all_r,
@@ -107,7 +109,11 @@
                         body(step, peer, peer // stride)
                 return carry
 
-            lax.fori_loop(1, n, one, 0)
+            if n <= 8:
+                for step in range(1, n):
+                    one(step, 0)
+            else:
+                lax.fori_loop(1, n, one, 0)
 
         def if_owner(axis, owners, body):
             me, n = place[axis], size[axis]
@@ -197,9 +203,38 @@
                         row * TILE - top:(row + 1) * TILE - top, col * TILE:(col + 1) * TILE]
 
         pl.semaphore_wait(barrier, n_img - 1 + n_blk - 1)
-        gram_scatter = scatter("img", 0, rows_gram, n_img, gram, gram_in, gram_s, gram_r)
-        gram_gather = gather("img", 0, rows_gram, n_img, gram_all, gram_all_s, gram_all_r)
-        gram_scatter[0]()
+
+        number, side = place["img"] // 2, lax.rem(place["img"], 2)
+        other = place["img"] + 1 - 2 * side
+
+        def to_device(source, target, send, recv, device):
+            return pltpu.make_async_remote_copy(
+                src_ref=source, dst_ref=target, send_sem=send, recv_sem=recv,
+                device_id={"img": device}, device_id_type=pl.DeviceIdType.MESH)
+
+        def each_pair(body):
+            for step in range(1, pairs):
+                peer = lax.rem(number + step, pairs)
+                body(step, peer, 2 * peer + side)
+
+        def gram_chunk(which):
+            return gram_all.at[span(side * half, which, rows_gram)]
+
+        def halves(from_side):
+            return to_device(gram.at[span(0, from_side, half)], gram_half, gram_s.at[0], gram_r.at[0], other)
+
+        def to_owner(step, peer, slot, device):
+            return to_device(gram_sum.at[span(0, peer, rows_gram)], gram_in.at[slot],
+                             gram_s.at[step], gram_r.at[1 + slot], device)
+
+        def to_all(step, chunk, device):
+            return to_device(gram_chunk(chunk), gram_chunk(chunk), gram_all_s.at[step], gram_all_r.at[chunk], device)
+
+        def to_other(chunk, at_side):
+            at = gram_all.at[span(at_side * half, chunk, rows_gram)]
+            return to_device(at, at, gram_all_s.at[pairs + chunk], gram_all_r.at[pairs + chunk], other)
+
+        halves(1 - side).start()
 
         def transfers(axis, turn, g, source, target, whole, sems):
             first, rows = groups[g]
@@ -271,13 +306,27 @@
                 out_weights[first:end, :] = w_all[step, first:end, :]
 
         every = range(len(groups))
-        for g in every:
+        begin_predict(0, 0, weights_ref[rows_of(0), :])
+        halves(side).wait_recv()
+        gram_sum[...] = gram[span(0, side, half), :] + gram_half[...]
+        each_pair(lambda step, peer, device: to_owner(step, peer, number, device).start())
+        gram_in[number] = gram_sum[span(0, number, rows_gram), :]
+        for g in every[1:]:
             begin_predict(0, g, weights_ref[rows_of(g), :])
-        gram_scatter[1]()
-        gram_gather[0](lambda mine: jnp.sum(gram_in[...], axis=0))
+        each_pair(lambda step, peer, device: to_owner(step, peer, peer, device).wait_recv())
+        gram_chunk(number)[...] = jnp.sum(gram_in[...], axis=0)
+        each_pair(lambda step, peer, device: to_all(step, number, device).start())
+        to_other(number, side).start()
         for g in every:
             middle_predict(0, g)
-        gram_gather[1]()
+
+        def pass_on(step, peer, device):
+            to_all(step, peer, device).wait_recv()
+            to_other(peer, side).start()
+
+        each_pair(pass_on)
+        for chunk in range(pairs):
+            to_other(chunk, 1 - side).wait_recv()
 
         diagonal = (lax.broadcasted_iota(jnp.int32, (TILE, TILE), 0)
                     == lax.broadcasted_iota(jnp.int32, (TILE, TILE), 1))
@@ -300,21 +349,19 @@
 
         def newton(step, carry):
             scale = scales_ref[step]
-            for top in range(0, filt, PANEL):
-                here = slice(top, top + PANEL)
-                y = dot_three(h_high[here, :], h_low[here, :], x_high[...], x_low[...])
-                same = (lax.broadcasted_iota(jnp.int32, y.shape, 0) + top
-                        == lax.broadcasted_iota(jnp.int32, y.shape, 1))
-                y_high[here, :], y_low[here, :] = split(jnp.where(same, 2.0, 0.0) - scale * y)
-            for top in range(0, filt, PANEL):
-                here = slice(top, top + PANEL)
-                x = dot_three(x_high[here, :], x_low[here, :], y_high[...], y_low[...])
-                x_high[here, :], x_low[here, :] = split(scale * x)
+            y = dot_three(h_high[...], h_low[...], x_high[...], x_low[...])
+            same = (lax.broadcasted_iota(jnp.int32, y.shape, 0)
+                    == lax.broadcasted_iota(jnp.int32, y.shape, 1))
+            y_high[...], y_low[...] = split(jnp.where(same, 2.0, 0.0) - scale * y)
+            x = dot_three(x_high[...], x_low[...], y_high[...], y_low[...])
+            x_high[...], x_low[...] = split(scale * x)
             return carry
 
+        begun = (len(scales) + 1) // 2
+        lax.fori_loop(1, begun, newton, 0)
         for g in every:
             end_predict(0, g)
-        lax.fori_loop(1, len(scales), newton, 0)
+        lax.fori_loop(begun, len(scales), newton, 0)
 
         stages = []
         for step in range(ITERS):
@@ -330,6 +377,11 @@
                     stages[tick - g](g)
         for wait_sent in unsent:
             wait_sent()
+        halves(1 - side).wait_send()
+        each_pair(lambda step, peer, device: to_owner(step, peer, number, device).wait_send())
+        each_pair(lambda step, peer, device: to_all(step, number, device).wait_send())
+        for chunk in range(pairs):
+            to_other(chunk, side).wait_send()
 
     f32, bf16 = jnp.float32, jnp.bfloat16
     square = (filt, filt)
@@ -338,7 +390,9 @@
     scratch = [
         pltpu.VMEM((filt, pos_pad), bf16),
         pltpu.VMEM((packed, TILE), f32),
-        pltpu.VMEM((n_img, rows_gram, TILE), f32),
+        pltpu.VMEM((half, TILE), f32),
+        pltpu.VMEM((half, TILE), f32),
+        pltpu.VMEM((pairs, rows_gram, TILE), f32),
         pltpu.VMEM((packed, TILE), f32),
         pltpu.VMEM(square, bf16), pltpu.VMEM(square, bf16),
         pltpu.VMEM(square, bf16), pltpu.VMEM(square, bf16),

time: 92.3 us -> 87.5 us (0.948)
  Pallas kernels: 85.2 us -> 80.3 us
    pallas_call x1, Pallas kernels: 85.2 us -> 80.3 us  [shards(): pl.pallas_call(kernel, out_shape=(jax.ShapeDtypeStruct((LABELS, filt), jn...]
where the time goes in v5:
time: 87.5 us; the launch traced here: 87.2 us
  Pallas kernels  80.3 us (92%)
  local copies, waits for them, and re-layouts  6.12 us (7%)
    pallas_call x1, Pallas kernels, shards(): pl.pallas_call(kernel, out_shape=(jax.ShapeDtypeStruct((LABELS, filt), jn...  80.3 us
    unnamed x17, local copies, waits for them, and re-layouts  3.45 us

profile of v5, /device:TPU:0, one launch (start us, length us, event | category | flops | bytes accessed | tf_op | source)
XLA Modules:
  0.0 87.2 jit_solution(10062558789704923637)
XLA Ops:
  0.6 1.3 %reshape.16 = bf16[4,28,14,128]{3,2,0,1:T(8,128)(2,1)S(1)} reshape(bf16[4,28,1792]{2,0,1:T(4,128)(2,1)} %param.6) | data formatting | bytes 802816 | tf_op jit(solution)/shard_map/reshape | solution.py:419
  1.9 0.2 pad_slice_fusion
  2.2 0.1 slice_dynamic-update-slice_fusion.4
  2.3 0.1 slice_dynamic-update-slice_fusion.3
  2.3 0.1 slice_dynamic-update-slice_fusion.2
  2.5 0.1 slice_dynamic-update-slice_fusion.1
  2.5 0.1 slice_dynamic-update-slice_fusion
  2.6 0.1 copy.10
  2.7 0.4 reshape.17
  3.1 0.0 copy-start.1
  3.1 0.1 pad.21.patches_ref
  3.2 1.0 %copy-done.1 = bf16[512,576]{0,1:T(8,128)(2,1)S(1)} copy-done((bf16[512,576]{0,1:T(8,128)(2,1)S(1)}, bf16[512,576]{0,1:T(8,128)(2,1)}, u32[]{:S(2)}) %copy-start.1) | copy-done | bytes 589848
  4.2 0.1 pad.22
  4.3 0.0 copy-start.4
  4.3 0.0 copy-start.3
  4.3 0.0 copy-start
  4.3 0.3 copy.11.filters_ref
  4.6 0.6 copy-done.2
  5.2 0.0 copy-done.4
  5.2 0.1 copy.12.phases_ref
  5.4 0.0 copy-done
  5.4 80.3 %shard_map.77 = (f32[150,512]{1,0:T(8,128)S(1)}, f32[150,784]{1,0:T(8,128)S(1)}) custom-call(bf16[896,768]{1,0:T(8,128)(2,1)S(1)} %pad.21.patches_ref, bf16[512,768]{1,0:T(8,128)(2,1)S(1)} %copy.11.filters_ref, f32[512,1]{1,0:T(8,128)S(1)} %copy.12.phases_ref, s32[1,896]{1,0:T(1,128)S(1)} %pad.23.labels_ref, f32[160,512]{1,0:T(8,128)S(1)} %pad.24.weights_ref, ...), custom_call_target="tpu_custom_call" | custom-call | tf_op jit(solution)/shard_map/pallas_call | solution.py:441
  85.7 0.7 copy.20
  86.4 0.8 copy.21
  (6 shorter events, 0.1 us)
Async XLA Ops:
  3.1 1.1 %copy-start.1 = (bf16[512,576]{0,1:T(8,128)(2,1)S(1)}, bf16[512,576]{0,1:T(8,128)(2,1)}, u32[]{:S(2)}) copy-start(bf16[512,576]{0,1:T(8,128)(2,1)} %param.7) | copy-start | bytes 1769476
  4.2 1.0 %copy-start.2 = (f32[150,512]{1,0:T(8,128)S(1)}, f32[150,512]{1,0:T(8,128)}, u32[]{:S(2)}) copy-start(f32[150,512]{1,0:T(8,128)} %param.10) | copy-start | bytes 921604
  4.3 0.9 %copy-start.4 = (f32[512]{0:T(512)S(1)}, f32[512]{0:T(512)}, u32[]{:S(2)}) copy-start(f32[512]{0:T(512)} %param.8) | copy-start | bytes 6148
  4.3 1.1 %copy-start.3 = (s32[784]{0:T(1024)S(1)}, s32[784]{0:T(1024)}, u32[]{:S(2)}) copy-start(s32[784]{0:T(1024)} %param.9) | copy-start | bytes 9412
  4.3 1.1 %copy-start = (f32[8]{0:T(128)S(1)}, f32[8]{0:T(128)}, u32[]{:S(2)}) copy-start(f32[8]{0:T(128)} %constant.9.clone.scales_ref) | copy-start | bytes 100

commit v6 on v5

--- a/solution.py
+++ b/solution.py
@@ -60,6 +60,7 @@
     unit = math.lcm(8 * n_img, 16 * n_blk)
     chunks = {"img": unit // n_img, "blk": unit // n_blk}
     last = math.lcm(*chunks.values())
+    unit = max(unit // 2, last)
     groups = []
     first = 0
     while first < LABELS:
@@ -306,13 +307,13 @@
                 out_weights[first:end, :] = w_all[step, first:end, :]
 
         every = range(len(groups))
-        begin_predict(0, 0, weights_ref[rows_of(0), :])
+        part[0] = (shrink * dot(weights_ref[...].astype(jnp.bfloat16), feat[...])).astype(jnp.bfloat16)
         halves(side).wait_recv()
         gram_sum[...] = gram[span(0, side, half), :] + gram_half[...]
         each_pair(lambda step, peer, device: to_owner(step, peer, number, device).start())
         gram_in[number] = gram_sum[span(0, number, rows_gram), :]
-        for g in every[1:]:
-            begin_predict(0, g, weights_ref[rows_of(g), :])
+        for g in every:
+            predict_transfers(0, g)[0]()
         each_pair(lambda step, peer, device: to_owner(step, peer, peer, device).wait_recv())
         gram_chunk(number)[...] = jnp.sum(gram_in[...], axis=0)
         each_pair(lambda step, peer, device: to_all(step, number, device).start())
@@ -360,7 +361,13 @@
         begun = (len(scales) + 1) // 2
         lax.fori_loop(1, begun, newton, 0)
         for g in every:
-            end_predict(0, g)
+            predict_transfers(0, g)[3]()
+        classes = lax.broadcasted_iota(jnp.int32, (rows_all, pos_pad), 0)
+        targets = jnp.where(labels_ref[...] == classes, 1.0, 0.0)
+        residual = targets - part_all[0].astype(jnp.float32)
+        proj[0] = dot_nt(residual.astype(jnp.bfloat16), feat[...])
+        for g in every:
+            project_transfers(0, g)[0]()
         lax.fori_loop(begun, len(scales), newton, 0)
 
         stages = []

time: 87.5 us -> 94.1 us (1.075)
  Pallas kernels: 80.3 us -> 86.9 us
    pallas_call x1, Pallas kernels: 80.3 us -> 86.9 us  [shards(): pl.pallas_call(kernel, out_shape=(jax.ShapeDtypeStruct((LABELS, filt), jn...]
where the time goes in v6:
time: 94.1 us; the launch traced here: 93.8 us
  Pallas kernels  86.9 us (92%)
  local copies, waits for them, and re-layouts  6.12 us (7%)
    pallas_call x1, Pallas kernels, shards(): pl.pallas_call(kernel, out_shape=(jax.ShapeDtypeStruct((LABELS, filt), jn...  86.9 us
    unnamed x17, local copies, waits for them, and re-layouts  3.45 us

profile of v6, /device:TPU:0, one launch (start us, length us, event | category | flops | bytes accessed | tf_op | source)
XLA Modules:
  0.0 93.8 jit_solution(16730342646595083219)
XLA Ops:
  0.6 1.3 %reshape.16 = bf16[4,28,14,128]{3,2,0,1:T(8,128)(2,1)S(1)} reshape(bf16[4,28,1792]{2,0,1:T(4,128)(2,1)} %param.6) | data formatting | bytes 802816 | tf_op jit(solution)/shard_map/reshape | solution.py:426
  1.9 0.2 pad_slice_fusion
  2.2 0.1 slice_dynamic-update-slice_fusion.4
  2.3 0.1 slice_dynamic-update-slice_fusion.3
  2.3 0.1 slice_dynamic-update-slice_fusion.2
  2.5 0.1 slice_dynamic-update-slice_fusion.1
  2.5 0.1 slice_dynamic-update-slice_fusion
  2.6 0.1 copy.10
  2.7 0.4 reshape.17
  3.1 0.0 copy-start.1
  3.1 0.1 pad.21.patches_ref
  3.2 1.0 %copy-done.1 = bf16[512,576]{0,1:T(8,128)(2,1)S(1)} copy-done((bf16[512,576]{0,1:T(8,128)(2,1)S(1)}, bf16[512,576]{0,1:T(8,128)(2,1)}, u32[]{:S(2)}) %copy-start.1) | copy-done | bytes 589848
  4.2 0.1 pad.22
  4.3 0.0 copy-start.4
  4.3 0.0 copy-start.3
  4.3 0.0 copy-start
  4.3 0.3 copy.11.filters_ref
  4.6 0.6 copy-done.2
  5.2 0.0 copy-done.4
  5.2 0.1 copy.12.phases_ref
  5.4 0.0 copy-done.3
  5.4 86.9 %shard_map.77 = (f32[150,512]{1,0:T(8,128)S(1)}, f32[150,784]{1,0:T(8,128)S(1)}) custom-call(bf16[896,768]{1,0:T(8,128)(2,1)S(1)} %pad.21.patches_ref, bf16[512,768]{1,0:T(8,128)(2,1)S(1)} %copy.11.filters_ref, f32[512,1]{1,0:T(8,128)S(1)} %copy.12.phases_ref, s32[1,896]{1,0:T(1,128)S(1)} %pad.23.labels_ref, f32[160,512]{1,0:T(8,128)S(1)} %pad.24.weights_ref, ...), custom_call_target="tpu_custom_call" | custom-call | tf_op jit(solution)/shard_map/pallas_call | solution.py:448
  92.3 0.7 copy.20
  93.0 0.8 copy.21
  (6 shorter events, 0.1 us)
Async XLA Ops:
  3.1 1.1 %copy-start.1 = (bf16[512,576]{0,1:T(8,128)(2,1)S(1)}, bf16[512,576]{0,1:T(8,128)(2,1)}, u32[]{:S(2)}) copy-start(bf16[512,576]{0,1:T(8,128)(2,1)} %param.7) | copy-start | bytes 1769476
  4.2 1.0 %copy-start.2 = (f32[150,512]{1,0:T(8,128)S(1)}, f32[150,512]{1,0:T(8,128)}, u32[]{:S(2)}) copy-start(f32[150,512]{1,0:T(8,128)} %param.10) | copy-start | bytes 921604
  4.3 0.9 copy-start.4
  4.3 1.1 %copy-start.3 = (s32[784]{0:T(1024)S(1)}, s32[784]{0:T(1024)}, u32[]{:S(2)}) copy-start(s32[784]{0:T(1024)} %param.9) | copy-start | bytes 9412
  4.3 1.1 %copy-start = (f32[8]{0:T(128)S(1)}, f32[8]{0:T(128)}, u32[]{:S(2)}) copy-start(f32[8]{0:T(128)} %constant.9.clone.scales_ref) | copy-start | bytes 100

commit v7 on v6

--- a/solution.py
+++ b/solution.py
@@ -60,7 +60,6 @@
     unit = math.lcm(8 * n_img, 16 * n_blk)
     chunks = {"img": unit // n_img, "blk": unit // n_blk}
     last = math.lcm(*chunks.values())
-    unit = max(unit // 2, last)
     groups = []
     first = 0
     while first < LABELS:

time: 94.1 us -> 86.6 us (0.920)
  Pallas kernels: 86.9 us -> 79.4 us
    pallas_call x1, Pallas kernels: 86.9 us -> 79.4 us  [shards(): pl.pallas_call(kernel, out_shape=(jax.ShapeDtypeStruct((LABELS, filt), jn...]
where the time goes in v7:
time: 86.6 us; the launch traced here: 86.3 us
  Pallas kernels  79.4 us (92%)
  local copies, waits for them, and re-layouts  6.12 us (7%)
    pallas_call x1, Pallas kernels, shards(): pl.pallas_call(kernel, out_shape=(jax.ShapeDtypeStruct((LABELS, filt), jn...  79.4 us
    unnamed x17, local copies, waits for them, and re-layouts  3.45 us

profile of v7, /device:TPU:0, one launch (start us, length us, event | category | flops | bytes accessed | tf_op | source)
XLA Modules:
  0.0 86.3 jit_solution(5933142684604877814)
XLA Ops:
  0.6 1.3 %reshape.16 = bf16[4,28,14,128]{3,2,0,1:T(8,128)(2,1)S(1)} reshape(bf16[4,28,1792]{2,0,1:T(4,128)(2,1)} %param.6) | data formatting | bytes 802816 | tf_op jit(solution)/shard_map/reshape | solution.py:425
  1.9 0.2 pad_slice_fusion
  2.2 0.1 slice_dynamic-update-slice_fusion.4
  2.3 0.1 slice_dynamic-update-slice_fusion.3
  2.3 0.1 slice_dynamic-update-slice_fusion.2
  2.5 0.1 slice_dynamic-update-slice_fusion.1
  2.5 0.1 slice_dynamic-update-slice_fusion
  2.6 0.1 copy.10
  2.7 0.4 reshape.17
  3.1 0.0 copy-start.1
  3.1 0.1 pad.21.patches_ref
  3.2 1.0 %copy-done.1 = bf16[512,576]{0,1:T(8,128)(2,1)S(1)} copy-done((bf16[512,576]{0,1:T(8,128)(2,1)S(1)}, bf16[512,576]{0,1:T(8,128)(2,1)}, u32[]{:S(2)}) %copy-start.1) | copy-done | bytes 589848
  4.2 0.1 pad.22
  4.3 0.0 copy-start.4
  4.3 0.0 copy-start.3
  4.3 0.0 copy-start
  4.3 0.3 copy.11.filters_ref
  4.6 0.6 copy-done.2
  5.2 0.0 copy-done.4
  5.2 0.1 copy.12.phases_ref
  5.4 0.0 copy-done.3
  5.4 79.4 %shard_map.77 = (f32[150,512]{1,0:T(8,128)S(1)}, f32[150,784]{1,0:T(8,128)S(1)}) custom-call(bf16[896,768]{1,0:T(8,128)(2,1)S(1)} %pad.21.patches_ref, bf16[512,768]{1,0:T(8,128)(2,1)S(1)} %copy.11.filters_ref, f32[512,1]{1,0:T(8,128)S(1)} %copy.12.phases_ref, s32[1,896]{1,0:T(1,128)S(1)} %pad.23.labels_ref, f32[160,512]{1,0:T(8,128)S(1)} %pad.24.weights_ref, ...), custom_call_target="tpu_custom_call" | custom-call | tf_op jit(solution)/shard_map/pallas_call | solution.py:447
  84.8 0.7 copy.20
  85.5 0.8 copy.21
  (6 shorter events, 0.1 us)
Async XLA Ops:
  3.1 1.1 %copy-start.1 = (bf16[512,576]{0,1:T(8,128)(2,1)S(1)}, bf16[512,576]{0,1:T(8,128)(2,1)}, u32[]{:S(2)}) copy-start(bf16[512,576]{0,1:T(8,128)(2,1)} %param.7) | copy-start | bytes 1769476
  4.2 1.0 %copy-start.2 = (f32[150,512]{1,0:T(8,128)S(1)}, f32[150,512]{1,0:T(8,128)}, u32[]{:S(2)}) copy-start(f32[150,512]{1,0:T(8,128)} %param.10) | copy-start | bytes 921604
  4.3 0.9 %copy-start.4 = (f32[512]{0:T(512)S(1)}, f32[512]{0:T(512)}, u32[]{:S(2)}) copy-start(f32[512]{0:T(512)} %param.8) | copy-start | bytes 6148
  4.3 1.1 %copy-start.3 = (s32[784]{0:T(1024)S(1)}, s32[784]{0:T(1024)}, u32[]{:S(2)}) copy-start(s32[784]{0:T(1024)} %param.9) | copy-start | bytes 9412
  4.3 1.1 %copy-start = (f32[8]{0:T(128)S(1)}, f32[8]{0:T(128)}, u32[]{:S(2)}) copy-start(f32[8]{0:T(128)} %constant.9.clone.scales_ref) | copy-start | bytes 100
